TPU v7x, 256 devices: a whole 4x4x8 slice. The times are simulated.
256 devices in a mesh: req: 16 (over y_hi, z), tp: 8 (over x, core), pp: 2 (over y_lo).
Axes of the slice: x: 4, y: 4 (y_hi: 2, y_lo: 2; y = y_hi * 2 + y_lo), z: 8, core: 2. Of those that a mesh axis runs over, the one named last changes fastest.
Arguments:
- prompt_states: bfloat16 [32, 128, 8192], P('tp', 'req', 'pp'), may hold values from -6 to 6
- prompt_lengths: int32 [32], replicated, may hold values from 1 to 128, 2560 in all
- adapter_ids: int32 [32], replicated, may hold values from 0 to 15
- w_query: bfloat16 [8192, 8192], P('pp', 'req'), may hold values from -2 to 2
- w_key: bfloat16 [8192, 1024], P('pp', 'req'), may hold values from -2 to 2
- value_weight: bfloat16 [8192, 1024], P('pp', 'req'), may hold values from -0.0625 to 0.0625
- down_query: bfloat16 [16, 8192, 32], P('req', 'pp'), may hold values from -0.0625 to 0.0625
- up_query: bfloat16 [16, 32, 8192], P(None, None, 'req'), may hold values from -1 to 1
- down_value: bfloat16 [16, 8192, 32], P('req', 'pp'), may hold values from -0.0625 to 0.0625
- value_up_weight: bfloat16 [16, 32, 1024], P(None, None, 'req'), may hold values from -1 to 1
- step_queries: bfloat16 [32, 4, 8192], P(('req', 'pp')), may hold values from -6 to 6
- step_keyvals: bfloat16 [32, 4, 2, 1024], P(('req', 'pp')), may hold values from -6 to 6
Outputs:
- prefill_out: bfloat16 [32, 128, 8192], P('tp', 'pp', 'req')
- decoded: bfloat16 [32, 4, 8192], P(('req', 'pp'))
Inputs may be any that keep to these rules, and one draw needn't show every extreme that they name: `prompt_lengths`: some prompt holds exactly 128 tokens.
All inputs are finite; a program needn't handle non-finite values.
Results may differ from a plain program's by a relative error of at most 0.011.
Values may be sent and summed in bfloat16 or wider, within the bound.
A program may use at most 64 MiB of HBM per device.

v0:
```python
import jax
import jax.numpy as jnp
from jax import lax
from jax.sharding import PartitionSpec as P

HEAD_SIZE = 128


NEG = -1e30


def partner(block, axis, apart):
    count = lax.axis_size(axis)
    route = []
    for low in range(count):
        high = low | 1 << apart
        if high != low and high < count:
            route += [(low, high), (high, low)]
    return lax.ppermute(block, axis, route)


def joined(value, axis, join):
    pieces = jax.tree.map(lambda part: lax.all_gather(part, axis), value)
    head = jax.tree.map(lambda part: part[0], pieces)
    tail = jax.tree.map(lambda part: part[1:], pieces)
    total, _ = lax.scan(lambda total, section: (join(total, section), None), head, tail)
    return total


def combine_partial(first, second):
    top = jnp.maximum(first[0], second[0])
    scale_one = jnp.exp(first[0] - top)
    scale_two = jnp.exp(second[0] - top)
    total = first[1] * scale_one + second[1] * scale_two
    summed = first[2] * scale_one[..., None] + second[2] * scale_two[..., None]
    return (top, total, summed)


def local(
    prompt_states,
    prompt_lengths,
    adapter_ids,
    w_query,
    w_key,
    value_weight,
    down_query,
    up_query,
    down_value,
    value_up_weight,
    step_queries,
    step_keyvals,
):
    single_float = jnp.float32
    bf16 = jnp.bfloat16
    req_count = lax.axis_size("req")
    tp_count = lax.axis_size("tp")
    pp_count = lax.axis_size("pp")
    req_index = lax.axis_index("req")
    tp_index = lax.axis_index("tp")
    pp_index = lax.axis_index("pp")
    prompt_block, pos_block, half_width = prompt_states.shape
    seq_len = pos_block * req_count
    query_cols = w_query.shape[1]
    kv_cols = w_key.shape[1]
    rank = down_query.shape[2]
    scale = HEAD_SIZE ** (-0.5)
    first_prompt = tp_index * prompt_block
    my_lengths = lax.dynamic_slice_in_dim(prompt_lengths, first_prompt, prompt_block)
    my_adapters = lax.dynamic_slice_in_dim(adapter_ids, first_prompt, prompt_block)
    table_query, table_value = (
        lax.all_gather(down_query, "req", axis=0, tiled=True),
        lax.all_gather(down_value, "req", axis=0, tiled=True),
    )
    rank_query = jnp.take(table_query, my_adapters, axis=0)
    rank_value = jnp.take(table_value, my_adapters, axis=0)
    piece = lax.all_gather(prompt_states, "req", axis=1, tiled=True)
    count = piece.shape[1]
    flat = piece.reshape(prompt_block * count, half_width)
    base_query = jnp.dot(flat, w_query, preferred_element_type=single_float)
    base_key = jnp.dot(flat, w_key, preferred_element_type=single_float)
    base_value = jnp.dot(flat, value_weight, preferred_element_type=single_float)
    dense = jnp.concatenate([base_query, base_key, base_value], axis=1).reshape(
        prompt_block, count, -1
    )
    low_query = jnp.einsum("pnd,pdr->pnr", piece, rank_query, preferred_element_type=single_float)
    low_value = jnp.einsum("pnd,pdr->pnr", piece, rank_value, preferred_element_type=single_float)
    packed = jnp.concatenate([dense, low_query, low_value], axis=2)
    query_part = packed[:, :, :query_cols]
    kv_part = packed[:, :, query_cols : query_cols + 2 * kv_cols]
    low_part = packed[:, :, query_cols + 2 * kv_cols :]
    query_sum, kv_sum, low_sum = lax.psum((query_part, kv_part, low_part), "pp")
    query_len = query_sum.shape[1]
    low_query = low_sum[:, :, :rank].astype(bf16)
    low_value = low_sum[:, :, rank:].astype(bf16)
    up_query_rows = jnp.take(up_query, my_adapters, axis=0)
    up_value_rows = jnp.take(value_up_weight, my_adapters, axis=0)
    query_rows = (
        query_sum
        + jnp.einsum("pnr,prc->pnc", low_query, up_query_rows, preferred_element_type=single_float)
    ).astype(bf16)
    keys_own = kv_sum[:, :, :kv_cols].astype(bf16)
    values_own = (
        kv_sum[:, :, kv_cols:]
        + jnp.einsum("pnr,prc->pnc", low_value, up_value_rows, preferred_element_type=single_float)
    ).astype(bf16)
    keys_all = keys_own
    values_all = values_own
    other_keys, other_values = partner((keys_all, values_all), "req", 0)
    upper = req_index // 2**0 % 2 == 1
    keys_all = jnp.where(
        upper,
        jnp.concatenate([other_keys, keys_all], axis=2),
        jnp.concatenate([keys_all, other_keys], axis=2),
    )
    values_all = jnp.where(
        upper,
        jnp.concatenate([other_values, values_all], axis=2),
        jnp.concatenate([values_all, other_values], axis=2),
    )
    local_kv = keys_all.shape[2] // HEAD_SIZE
    local_query = query_cols // HEAD_SIZE
    per_kv = local_query // local_kv
    query_heads = query_rows.reshape(prompt_block, query_len, local_kv, per_kv, HEAD_SIZE)
    key_heads = keys_all.reshape(prompt_block, seq_len, local_kv, HEAD_SIZE)
    value_heads = values_all.reshape(prompt_block, seq_len, local_kv, HEAD_SIZE)
    scores = (
        jnp.einsum("pikgd,pjkd->pkgij", query_heads, key_heads, preferred_element_type=single_float)
        * scale
    )
    rows = jnp.arange(query_len, dtype=jnp.int32)
    cols = jnp.arange(seq_len, dtype=jnp.int32)
    allowed = (cols[None, None, :] <= rows[None, :, None]) & (
        cols[None, None, :] < my_lengths[:, None, None]
    )
    scores = jnp.where(allowed[:, None, None], scores, NEG)
    top = jnp.max(scores, axis=-1, keepdims=True)
    raised = jnp.exp(scores - top)
    weights = (raised / jnp.sum(raised, axis=-1, keepdims=True)).astype(bf16)
    mixed = jnp.einsum(
        "pkgij,pjkd->pikgd", weights, value_heads, preferred_element_type=single_float
    )
    live_rows = rows[None, :] < my_lengths[:, None]
    mixed = jnp.where(live_rows[:, :, None, None, None], mixed, 0.0)
    mixed = mixed.reshape(prompt_block, query_len, query_cols).astype(bf16)
    share = seq_len // pp_count
    prefill_out = lax.dynamic_slice_in_dim(mixed, pp_index * share, share, 1)
    pos_share = seq_len // (tp_count * pp_count)
    stacked = jnp.stack([keys_own, values_own], axis=2)
    stacked = stacked.reshape(prompt_block, tp_count, pp_count, pos_share, 2, kv_cols)
    own_slots = lax.dynamic_index_in_dim(stacked, pp_index, 2, keepdims=False)
    cache = lax.all_to_all(
        lax.all_to_all(own_slots, "tp", split_axis=1, concat_axis=0, tiled=True),
        ("req", "pp"),
        split_axis=0,
        concat_axis=1,
        tiled=True,
    )
    req_dev = step_queries.shape[0]
    steps = step_queries.shape[1]
    cache = cache.reshape(req_dev, req_count, pp_count, pos_share, 2, kv_cols)
    block_len = pp_count * pos_share
    cache = cache.transpose(0, 4, 2, 3, 1, 5).reshape(req_dev, 2, block_len, req_count * kv_cols)
    first_request = (req_index * pp_count + pp_index) * req_dev
    request_lengths = lax.dynamic_slice_in_dim(prompt_lengths, first_request, req_dev)
    heads_kv = cache.shape[3] // HEAD_SIZE
    head_group = step_queries.shape[2] // cache.shape[3]
    step_heads = step_queries.reshape(req_dev, steps, heads_kv, head_group, HEAD_SIZE)
    cached_keys = cache[:, 0].reshape(req_dev, block_len, heads_kv, HEAD_SIZE)
    cached_values = (
        cache[:, 1].reshape(req_dev, block_len, heads_kv, HEAD_SIZE).astype(single_float)
    )
    positions = tp_index * block_len + jnp.arange(block_len, dtype=jnp.int32)
    live = (positions[None, :] < request_lengths[:, None])[:, None, None, None, :]
    old_scores = (
        jnp.einsum(
            "nskgd,nckd->nkgsc", step_heads, cached_keys, preferred_element_type=single_float
        )
        * scale
    )
    old_scores = jnp.where(live, old_scores, NEG)
    old_top = jnp.max(old_scores, axis=-1)
    old_raised = jnp.where(live, jnp.exp(old_scores - old_top[..., None]), 0.0)
    old_total = jnp.sum(old_raised, axis=-1)
    old_summed = jnp.einsum(
        "nkgsc,nckd->nkgsd", old_raised, cached_values, precision=lax.Precision.HIGHEST
    )
    top_all, total_all, summed_all = joined((old_top, old_total, old_summed), "tp", combine_partial)
    new_keys = step_keyvals[:, :, 0].reshape(req_dev, steps, heads_kv, HEAD_SIZE)
    new_values = (
        step_keyvals[:, :, 1].astype(single_float).reshape(req_dev, steps, heads_kv, HEAD_SIZE)
    )
    new_scores = (
        jnp.einsum("nskgd,ntkd->nkgst", step_heads, new_keys, preferred_element_type=single_float)
        * scale
    )
    causal = jnp.arange(steps)[None, :] <= jnp.arange(steps)[:, None]
    new_scores = jnp.where(causal, new_scores, NEG)
    final_top = jnp.maximum(top_all, jnp.max(new_scores, axis=-1))
    old_scale = jnp.exp(top_all - final_top)
    new_raised = jnp.where(causal, jnp.exp(new_scores - final_top[..., None]), 0.0)
    total_final = total_all * old_scale + jnp.sum(new_raised, axis=-1)
    summed_final = summed_all * old_scale[..., None] + jnp.einsum(
        "nkgst,ntkd->nkgsd", new_raised, new_values, precision=lax.Precision.HIGHEST
    )
    decoded = (
        (summed_final / total_final[..., None])
        .transpose(0, 3, 1, 2, 4)
        .reshape(req_dev, steps, step_queries.shape[2])
        .astype(bf16)
    )
    return (prefill_out, decoded)


def solution(mesh):
    in_specs = (
        P("tp", "req", "pp"),
        P(),
        P(),
        P("pp", "req"),
        P("pp", "req"),
        P("pp", "req"),
        P("req", "pp", None),
        P(None, None, "req"),
        P("req", "pp", None),
        P(None, None, "req"),
        P(("req", "pp"), None, None),
        P(("req", "pp"), None, None, None),
    )
    out_specs = (P("tp", "pp", "req"), P(("req", "pp"), None, None))
    return jax.shard_map(local, mesh=mesh, in_specs=in_specs, out_specs=out_specs, check_vma=False)
```

profile of v0, /device:TPU:1, one launch (start us, length us, event | category | flops | bytes accessed | tf_op | source)
XLA Modules:
  0.0 455.7 jit_solution(4399709015090550969)
XLA Ops:
  9.5 0.7 dynamic_slice.27
  10.9 1.5 gather_fusion
  12.4 98.9 %all-gather.8.cloned.1.call-done = bf16[4,128,4096]{2,1,0:T(8,128)(2,1)} async-done(((bf16[4,8,4096]{2,1,0:T(8,128)(2,1)}), bf16[4,128,4096]{2,1,0:T(8,128)(2,1)}) %all-gather.8.cloned.1.call-update) | async-done | bytes 4194320 | tf_op jit(solution)/shard_map/all_gather | solution.py:76
  111.3 3.8 fusion.90
  115.2 1.4 fusion.91
  116.6 2.4 fusion.89
  119.6 1.3 copy.96
  121.8 88.6 %all-gather.12.cloned.1.call-done = bf16[16,4096,32]{1,2,0:T(8,128)(2,1)} async-done(((bf16[1,4096,32]{1,2,0:T(8,128)(2,1)}), bf16[16,4096,32]{1,2,0:T(8,128)(2,1)}) %all-gather.12.cloned.1.call-update) | async-done | bytes 4194320 | tf_op jit(solution)/shard_map/all_gather | solution.py:72
  210.4 2.8 gather_fusion.3
  213.2 96.3 %all-gather.10.cloned.1.call-done = bf16[16,4096,32]{1,2,0:T(8,128)(2,1)} async-done(((bf16[1,4096,32]{1,2,0:T(8,128)(2,1)}), bf16[16,4096,32]{1,2,0:T(8,128)(2,1)}) %all-gather.10.cloned.1.call-update) | async-done | bytes 4194320 | tf_op jit(solution)/shard_map/all_gather | solution.py:71
  309.6 2.8 gather_fusion.2
  312.4 3.8 convolution_bitcast_fusion.2
  316.3 1.5 convolution_bitcast_fusion.3
  317.8 6.8 %all-reduce.5 = bf16[4,128,64]{1,2,0:T(8,128)(2,1)S(1)} all-reduce(f32[4,128,64]{1,2,0:T(8,128)S(1)} %pad_maximum_fusion.1), channel_id=1, replica_groups=mesh['req'=16,'tp'=8,'pp'=2] {'pp'}, use_global_device_ids=true, to_apply=%region_1.3 | all-reduce | flops 32768 | bytes 196608 | tf_op jit(solution)/shard_map/psum | solution.py:91
  324.6 46.1 %all-reduce.4.cloned.1.call-done = (f32[4,128,512]{2,1,0:T(8,128)}, f32[4,128,128]{1,2,0:T(8,128)}) async-done(((f32[4,128,512]{2,1,0:T(8,128)}, f32[4,128,128]{1,2,0:T(8,128)}), (f32[4,128,512]{2,1,0:T(8,128)}, f32[4,128,128]{1,2,0:T(8,128)})) %all-reduce.4.cloned.1.call-update) | async-done | bytes 1310736 | tf_op jit(solution)/shard_map/psum | solution.py:91
  370.7 1.0 slice.108
  371.7 1.2 fusion.16
  373.2 0.8 reshape.325
  374.0 4.9 %all-to-all-start = ((bf16[8,2,2048]{2,1,0:T(2,128)(2,1)}), bf16[8,2,2048]{2,1,0:T(2,128)(2,1)S(1)}, u32[]{:S(2)}, u32[]{:S(2)}) async-start(bf16[8,2,2048]{2,1,0:T(2,128)(2,1)} %reshape.325), calls=%async_computation | async-start | bytes 131072 | tf_op jit(solution)/shard_map/all_to_all | solution.py:152
  379.7 4.1 all-to-all-done
  383.9 0.8 reshape.327
  384.7 9.3 %all-to-all-start.1 = ((bf16[32,2,512]{2,1,0:T(2,128)(2,1)}), bf16[32,2,512]{2,1,0:T(2,128)(2,1)S(1)}, u32[]{:S(2)}, u32[]{:S(2)}) async-start(bf16[32,2,512]{2,1,0:T(2,128)(2,1)} %reshape.327), calls=%async_computation.1 | async-start | bytes 131072 | tf_op jit(solution)/shard_map/all_to_all | solution.py:151
  394.8 8.5 %all-to-all-done.1 = bf16[32,2,512]{2,1,0:T(2,128)(2,1)S(1)} async-done(((bf16[32,2,512]{2,1,0:T(2,128)(2,1)}), bf16[32,2,512]{2,1,0:T(2,128)(2,1)S(1)}, u32[]{:S(2)}, u32[]{:S(2)}) %all-to-all-start.1) | async-done | bytes 65568 | tf_op jit(solution)/shard_map/all_to_all | solution.py:151
  403.9 0.9 fusion.48
  406.4 1.1 collective-permute-start
  407.8 1.3 collective-permute-done.1
  410.4 0.9 copy.97
  411.5 15.9 %all-gather.1 = f32[64,8,4]{1,2,0:T(4,128)S(1)} all-gather(f32[8,8,4]{1,2,0:T(4,128)S(1)} %fusion.54), channel_id=3, replica_groups=mesh['req'=16,'tp'=8,'pp'=2] {'tp'}, dimensions={0}, use_global_device_ids=true | all-gather | bytes 9216 | tf_op jit(solution)/shard_map/all_gather | solution.py:23
  427.5 12.8 %all-gather = f32[64,8,4]{1,2,0:T(4,128)S(1)} all-gather(f32[8,8,4]{1,2,0:T(4,128)S(1)} %get-tuple-element.96), channel_id=2, replica_groups=mesh['req'=16,'tp'=8,'pp'=2] {'tp'}, dimensions={0}, use_global_device_ids=true | all-gather | bytes 9216 | tf_op jit(solution)/shard_map/all_gather | solution.py:23
  440.3 0.9 slice_bitcast_fusion
  441.3 1.2 slice.94
  442.5 5.4 %while.14 = (s32[]{:T(128)}, f32[1,8,8,4]{2,3,1,0:T(4,128)S(1)}, f32[1,8,8,4]{2,3,1,0:T(4,128)S(1)}, f32[1,8,8,4,128]{4,3,2,1,0:T(4,128)S(1)}, f32[7,1,8,8,4]{3,...) while((s32[]{:T(128)}, f32[1,8,8,4]{2,3,1,0:T(4,128)S(1)}, ...), condition=%wide.region_8.10_spmd, body=%wide.region_7.9_spmd.sunk | while | flops 100098 | bytes 674913 | solution.py:26
  (127 shorter events, 16.7 us)
Async XLA Ops:
  7.2 397.8 %copy-start = (bf16[16,32,512]{2,1,0:T(8,128)(2,1)S(1)}, bf16[16,32,512]{2,1,0:T(8,128)(2,1)}, u32[]{:S(2)}) copy-start(bf16[16,32,512]{2,1,0:T(8,128)(2,1)} %param.23) | copy-start | bytes 1572868
  7.2 108.0 %copy-start.4 = (bf16[4096,64]{0,1:T(8,128)(2,1)S(1)}, bf16[4096,64]{0,1:T(8,128)(2,1)}, u32[]{:S(2)}) copy-start(bf16[4096,64]{0,1:T(8,128)(2,1)} %param.21) | copy-start | bytes 1572868
  7.2 104.1 %all-gather.8.cloned.1.call-start = ((), (), s32[]{:S(2)}) async-start(), calls=%async_computation.2 | async-start | bytes 4456448 | tf_op jit(solution)/shard_map/all_gather | solution.py:76
  7.9 202.5 %all-gather.12.cloned.1.call-start = ((), (), s32[]{:S(2)}) async-start(), calls=%async_computation.4 | async-start | bytes 4456448 | tf_op jit(solution)/shard_map/all_gather | solution.py:72
  8.7 300.9 %all-gather.10.cloned.1.call-start = ((), (), s32[]{:S(2)}) async-start(), calls=%async_computation.3 | async-start | bytes 4456448 | tf_op jit(solution)/shard_map/all_gather | solution.py:71
  9.4 361.3 %all-reduce.4.cloned.1.call-start = ((), (), s32[]{:S(2)}) async-start(), calls=%async_computation.6 | async-start | bytes 2621440 | tf_op jit(solution)/shard_map/psum | solution.py:91
  111.3 3.9 copy-start.1
  111.3 5.3 %copy-start.6 = (bf16[4096,512]{1,0:T(8,128)(2,1)S(1)}, bf16[4096,512]{1,0:T(8,128)(2,1)}, u32[]{:S(2)}) copy-start(bf16[4096,512]{1,0:T(8,128)(2,1)} %param.19) | copy-start | bytes 12582916
  312.4 3.9 copy-start.2
  316.2 62.9 %copy-start.8 = (s32[32]{0:T(128)S(1)}, s32[32]{0:T(128)}, u32[]{:S(2)}) copy-start(s32[32]{0:T(128)} %param.17) | copy-start | bytes 388
  316.2 78.5 %copy-start.5 = (bf16[1,4,2,1024]{3,2,1,0:T(2,128)(2,1)S(1)}, bf16[1,4,2,1024]{3,2,1,0:T(2,128)(2,1)}, u32[]{:S(2)}) copy-start(bf16[1,4,2,1024]{3,2,1,0:T(2,128)(2,1)} %param.27) | copy-start | bytes 49156
  316.3 87.4 %copy-start.7 = (bf16[1,4,8192]{2,1,0:T(4,128)(2,1)S(1)}, bf16[1,4,8192]{2,1,0:T(4,128)(2,1)}, u32[]{:S(2)}) copy-start(bf16[1,4,8192]{2,1,0:T(4,128)(2,1)} %param.26) | copy-start | bytes 196612
  370.7 36.8 %copy-start.3 = (f32[4,128,512]{2,1,0:T(8,128)S(1)}, f32[4,128,512]{2,1,0:T(8,128)}, u32[]{:S(2)}) copy-start(f32[4,128,512]{2,1,0:T(8,128)} %get-tuple-element.82) | copy-start | bytes 3145732
  374.0 9.8 %all-to-all-start = ((bf16[8,2,2048]{2,1,0:T(2,128)(2,1)}), bf16[8,2,2048]{2,1,0:T(2,128)(2,1)S(1)}, u32[]{:S(2)}, u32[]{:S(2)}) async-start(bf16[8,2,2048]{2,1,0:T(2,128)(2,1)} %reshape.325), calls=%async_computation | async-start | bytes 131072 | tf_op jit(solution)/shard_map/all_to_all | solution.py:152
  384.7 18.6 %all-to-all-start.1 = ((bf16[32,2,512]{2,1,0:T(2,128)(2,1)}), bf16[32,2,512]{2,1,0:T(2,128)(2,1)S(1)}, u32[]{:S(2)}, u32[]{:S(2)}) async-start(bf16[32,2,512]{2,1,0:T(2,128)(2,1)} %reshape.327), calls=%async_computation.1 | async-start | bytes 131072 | tf_op jit(solution)/shard_map/all_to_all | solution.py:151
  394.0 46.3 %all-gather.14.cloned.1.call-start = ((), (), s32[]{:S(2)}) async-start(), calls=%async_computation.5 | async-start | bytes 1179648 | tf_op jit(solution)/shard_map/all_gather | solution.py:23
  405.9 3.2 collective-permute-start.1
  406.4 3.5 collective-permute-start
Sparse Core Ops, SparseCore 0:
  10.6 100.6 all-gather.7
  113.9 96.4 all-gather.11
  213.0 96.4 all-gather.9
  312.6 58.0 all-reduce.3
  405.0 20.3 all-gather.13
where the time goes:
time: 456 us
  waiting for transfers between devices  346 us (76%)
  blocking collectives  35.5 us (8%)
  local copies, waits for them, and re-layouts  20.8 us (5%)
  matrix products  17.2 us (4%)
  starting transfers between devices  15.9 us (3%)
  between operations  14.2 us (3%)
  other arithmetic  5.67 us (1%)
    all_gather x1, waiting for transfers between devices, local(): piece = lax.all_gather(prompt_states, 'req', axis=1, tiled=True)  98.9 us
    all_gather x1, waiting for transfers between devices, local(): lax.all_gather(down_query, 'req', axis=0, tiled=True)  96.3 us
    all_gather x1, waiting for transfers between devices, local(): lax.all_gather(down_value, 'req', axis=0, tiled=True)  88.6 us
    psum x1, waiting for transfers between devices, local(): query_sum, kv_sum, low_sum = lax.psum((query_part, kv_part, low_part), 'pp')  46.1 us
    all_gather x2, blocking collectives, joined(): pieces = jax.tree.map(lambda part: lax.all_gather(part, axis), value)  28.7 us
    all_to_all x1, starting transfers between devices, local(): lax.all_to_all(lax.all_to_all(own_slots, 'tp', split_axis=1, concat_axis=...  9.28 us
  transfers between devices with their start and end apart: 9, of which 8 were waited for; matrix products, arithmetic and copies ran while one was open for 6% of the time, Pallas kernels for 0%

commit v1 on v0

v1 whole, which is shorter than its diff:
```python
import functools

import jax
import jax.numpy as jnp
from jax import lax
from jax.experimental import pallas as pl
from jax.experimental.pallas import tpu as pltpu
from jax.sharding import PartitionSpec as P

HEAD = 128
SLOTS = 8
SIDE = 256
NEG = -1e30
F32 = jnp.float32
BF16 = jnp.bfloat16
MESH = pl.DeviceIdType.MESH


def kernel(
    req_count,
    tp_count,
    lens,
    adapters,
    x_hbm,
    wq_hbm,
    wk_hbm,
    wv_hbm,
    dq_hbm,
    dv_hbm,
    uq_hbm,
    uv_hbm,
    msg_ref,
    prefill_ref,
    decoded_ref,
    blocks,
    weights,
    side_w,
    uq,
    uv,
    qbuf,
    qrecv,
    side,
    siderecv,
    kv_own,
    kvsend,
    kvrecv,
    lowsend,
    lowrecv,
    rank_all,
    uv_send,
    uv_recv,
    k_full,
    v_full,
    step_in,
    step_out,
    step_recv,
    load_sem,
    ring_send,
    ring_recv,
    q_send,
    q_recv,
    side_send,
    side_recv,
    kv_send,
    kv_recv,
    low_send,
    low_recv,
    rank_send,
    rank_recv,
    uv_sems,
    step_send,
    step_got,
    out_send,
    out_got,
):
    r, t, p = lax.axis_index("req"), lax.axis_index("tp"), lax.axis_index("pp")
    ring = req_count // 2
    h, z = r // ring, r % ring
    rows = x_hbm.shape[0]
    prompts = rows // SLOTS
    cols = qbuf.shape[3]
    heads = cols // HEAD
    per_dev = msg_ref.shape[0]
    above = h * ring + (z + 1) % ring
    below = h * ring + (z + ring - 1) % ring
    across = (1 - h) * ring + z
    other = 1 - p
    pair = r + 1 - 2 * (r % 2)

    def remote(src, dst, send, recv, req=None, tp=None, pp=None):
        where = (r if req is None else req, t if tp is None else tp, p if pp is None else pp)
        return pltpu.make_async_remote_copy(
            src_ref=src,
            dst_ref=dst,
            send_sem=send,
            recv_sem=recv,
            device_id=where,
            device_id_type=MESH,
        )

    loads = [
        pltpu.make_async_copy(src, dst, load_sem.at[i])
        for i, (src, dst) in enumerate(
            [
                (wk_hbm, side_w.at[pl.ds(0, wk_hbm.shape[0])]),
                (wv_hbm, side_w.at[pl.ds(wk_hbm.shape[0], wk_hbm.shape[0])]),
                (dq_hbm, side_w.at[pl.ds(2 * wk_hbm.shape[0], dq_hbm.shape[0])]),
                (
                    dv_hbm,
                    side_w.at[pl.ds(2 * wk_hbm.shape[0] + dq_hbm.shape[0], dq_hbm.shape[0])],
                ),
                (x_hbm, blocks.at[pl.ds(0, rows)]),
                (wq_hbm, weights),
                (uq_hbm, uq),
                (uv_hbm, uv),
            ]
        )
    ]
    for load in loads:
        load.start()

    barrier = pltpu.get_barrier_semaphore()
    for where in ((above, t, p), (below, t, p), (across, t, p), (r, t, other)):
        pl.semaphore_signal(barrier, inc=1, device_id=where, device_id_type=MESH)
    for o in range(1, tp_count):
        pl.semaphore_signal(
            barrier, inc=1, device_id=(r, (t + o) % tp_count, p), device_id_type=MESH
        )
    pl.semaphore_wait(barrier, 3 + tp_count)

    def block(b):
        return blocks.at[pl.ds(pl.multiple_of(b * rows, rows), rows)]

    def hop(b, src, req):
        return remote(src, block(b), ring_send.at[b], ring_recv.at[b], req=req)

    half = ring // 2
    last = 2 * ring - 2

    hop(1, x_hbm, across).start()
    hop(2, x_hbm, above).start()
    if half > 1:
        hop(3, x_hbm, below).start()

    kv_cols, rank = wk_hbm.shape[0], dq_hbm.shape[0]
    used = 2 * kv_cols + 2 * rank
    side_w[used:] = jnp.zeros((SIDE - used, side_w.shape[1]), BF16)
    for load in loads:
        load.wait()

    def project(c, places):
        a = blocks[pl.ds(pl.multiple_of(c * 2 * rows, 2 * rows), 2 * rows), :]
        for n in range(0, cols, 256):
            width = min(256, cols - n)
            got = jnp.dot(a, weights[:, n : n + width], preferred_element_type=F32)
            for i, (zz, hh) in enumerate(places):
                sent = jnp.where(hh == p, 0, 1)
                qbuf[sent, zz, :, n : n + width] = got[i * rows : (i + 1) * rows]
        got = lax.dot_general(
            a, side_w[...], (((1,), (1,)), ((), ())), preferred_element_type=F32
        )
        for i, (zz, hh) in enumerate(places):
            side[hh, zz] = got[i * rows : (i + 1) * rows]

    def q_copy(zz):
        return remote(qbuf.at[1, zz], qrecv.at[zz], q_send.at[zz], q_recv.at[zz], pp=other)

    def side_copy(zz):
        return remote(
            side.at[:, zz], siderecv.at[:, zz], side_send.at[zz], side_recv.at[zz], pp=other
        )

    def exchange(zz):
        side_copy(zz).start()
        q_copy(zz).start()

    def kv_copy(zz):
        return remote(
            kvsend.at[:, zz], kvrecv.at[:, zz], kv_send.at[zz], kv_recv.at[zz], req=pair
        )

    def low_copy(target):
        return remote(
            lowsend.at[target], lowrecv.at[r], low_send.at[target], low_recv.at[r], req=target
        )

    def low_arrival(source):
        return remote(
            lowsend.at[source], lowrecv.at[source], low_send.at[source], low_recv.at[source], req=source
        )

    prompt_of = lax.broadcasted_iota(jnp.int32, (rows, HEAD), 0) // SLOTS
    match = jnp.zeros((rows, HEAD), F32)
    for i in range(prompts):
        mine = jnp.where(adapters[t * prompts + i] == r, 1.0, 0.0)
        match = jnp.where(prompt_of == i, mine, match)

    def finish(zz, self_too):
        side_copy(zz).wait_recv()
        for hh in range(2):
            total = side[hh, zz] + siderecv[hh, zz]
            kv_own[hh, zz] = total[:, :HEAD]
            kvsend[hh, zz] = total[:, :HEAD].astype(BF16)
            low = jnp.where(match > 0.0, total[:, HEAD:SIDE], 0.0).astype(BF16)
            target = hh * ring + zz
            lowsend[target] = low
            if self_too:

                @pl.when(target == r)
                def _():
                    lowrecv[r] = low

                @pl.when(target != r)
                def _():
                    low_copy(target).start()
            else:
                low_copy(target).start()
        kv_copy(zz).start()

    hop(1, x_hbm, across).wait_recv()
    if half > 1:
        hop(4, block(1), above).start()
        hop(5, block(1), below).start()
    else:
        hop(3, block(1), below).start()

    project(0, [(z, h), (z, 1 - h)])
    exchange(z)

    def step(k, _):
        base = 2 + 4 * (k - 1)
        up, down = (z + ring - k) % ring, (z + k) % ring
        hop(base, x_hbm, above).wait_recv()
        hop(base + 4, block(base), above).start()
        hop(base + 1, x_hbm, below).wait_recv()

        @pl.when(k + 1 < half)
        def _():
            hop(base + 5, block(base + 1), below).start()

        project(1 + 2 * (k - 1), [(up, h), (down, h)])
        hop(base + 2, x_hbm, above).wait_recv()

        @pl.when(k + 1 < half)
        def _():
            hop(base + 6, block(base + 2), above).start()

        hop(base + 3, x_hbm, below).wait_recv()

        @pl.when(k + 1 < half)
        def _():
            hop(base + 7, block(base + 3), below).start()

        @pl.when(k + 1 == half)
        def _():
            hop(last + 1, block(base + 3), below).start()

        project(2 + 2 * (k - 1), [(up, 1 - h), (down, 1 - h)])
        exchange(up)
        exchange(down)

        @pl.when(k == 1)
        def _():
            finish(z, True)

        @pl.when(k > 1)
        def _():
            finish((z + ring - k + 1) % ring, False)
            finish((z + k - 1) % ring, False)

        return 0

    lax.fori_loop(1, half, step, 0)
    far = (z + half) % ring
    if half == 1:
        finish(z, True)
    else:
        finish((z + ring - half + 1) % ring, False)
        finish((z + half - 1) % ring, False)
    hop(last, x_hbm, above).wait_recv()
    hop(last + 1, x_hbm, below).wait_recv()
    project(ring - 1, [(far, h), (far, 1 - h)])
    exchange(far)

    def step_copy(i):
        target = t * per_dev + i
        return remote(
            msg_ref.at[i],
            step_in.at[r % per_dev],
            step_send.at[i],
            step_got.at[r % per_dev],
            req=target,
            tp=r // per_dev,
        )

    def step_self(i):
        return (t * per_dev + i == r) & (r // per_dev == t)

    for i in range(per_dev):

        @pl.when(step_self(i))
        def _():
            step_in[r % per_dev] = msg_ref[i]

        @pl.when(jnp.logical_not(step_self(i)))
        def _():
            step_copy(i).start()

    for i in range(prompts):
        uv_send[i] = uv[adapters[t * prompts + i]]
    uv_copy = remote(uv_send, uv_recv, uv_sems.at[0], uv_sems.at[1], req=pair)
    uv_copy.start()

    finish(far, False)

    def others(body):
        def one(o, _):
            body((r + o) % req_count)
            return 0

        lax.fori_loop(1, req_count, one, 0)

    others(lambda source: low_arrival(source).wait_recv())
    low = lowrecv[0].astype(F32)
    for source in range(1, req_count):
        low = low + lowrecv[source].astype(F32)
    rank_all[r] = low.astype(BF16)

    def rank_copy(target, slot):
        return remote(
            rank_all.at[slot], rank_all.at[slot], rank_send.at[target], rank_recv.at[slot], req=target
        )

    others(lambda target: rank_copy(target, r).start())

    for zz in range(ring):
        kv_copy(zz).wait_recv()
        q_copy(zz).wait_recv()
    uv_copy.wait_recv()
    others(lambda source: rank_copy(source, source).wait_recv())

    even = r % 2 == 0
    slots = req_count * SLOTS
    share = slots // 2
    own = kv_own[...].reshape(req_count, prompts, SLOTS, HEAD)
    oth = kvrecv[...].astype(F32).reshape(req_count, prompts, SLOTS, HEAD)
    ranks = rank_all[...].astype(F32).reshape(req_count, prompts, SLOTS, HEAD)
    base_q = (qbuf[0] + qrecv[...]).reshape(ring, prompts, SLOTS, cols)
    my_ranks = rank_all[pl.ds(p * ring, ring)].astype(F32).reshape(ring, prompts, SLOTS, HEAD)
    lane = lax.broadcasted_iota(jnp.int32, (slots, HEAD), 1)
    low_lane = lane < HEAD // 2
    scale = HEAD ** (-0.5)
    row_pos = lax.broadcasted_iota(jnp.int32, (heads * share, slots), 0) % share + p * share
    col_pos = lax.broadcasted_iota(jnp.int32, (heads * share, slots), 1)
    out_pos = lax.broadcasted_iota(jnp.int32, (heads * share, HEAD), 0) % share + p * share
    for i in range(prompts):
        length = lens[t * prompts + i]
        adapter = adapters[t * prompts + i]
        mine = own[:, i].reshape(slots, HEAD)
        theirs = oth[:, i].reshape(slots, HEAD)
        first = jnp.where(even, mine, theirs)
        second = jnp.where(even, theirs, mine)
        k = jnp.where(low_lane, first, pltpu.roll(second, HEAD // 2, 1)).astype(BF16)
        v_base = jnp.where(low_lane, pltpu.roll(first, HEAD // 2, 1), second)
        uv_mine, uv_theirs = uv_send[i], uv_recv[i]
        up_v = jnp.concatenate(
            [jnp.where(even, uv_mine, uv_theirs), jnp.where(even, uv_theirs, uv_mine)], axis=1
        )
        rank_rows = ranks[:, i].reshape(slots, HEAD).astype(BF16)
        v = v_base + jnp.dot(rank_rows[:, rank : 2 * rank], up_v, preferred_element_type=F32)
        v = v.astype(BF16)
        k_full[i] = k
        v_full[i] = v
        rank_q = my_ranks[:, i].reshape(share, HEAD).astype(BF16)[:, :rank]
        q = base_q[:, i].reshape(share, cols) + jnp.dot(
            rank_q, uq[adapter], preferred_element_type=F32
        )
        q = q.astype(BF16)
        q = jnp.concatenate([q[:, g * HEAD : (g + 1) * HEAD] for g in range(heads)], axis=0)
        s = lax.dot_general(q, k, (((1,), (1,)), ((), ())), preferred_element_type=F32) * scale
        s = jnp.where((col_pos <= row_pos) & (col_pos < length), s, NEG)
        e = jnp.exp(s - jnp.max(s, axis=1, keepdims=True))
        w = (e / jnp.sum(e, axis=1, keepdims=True)).astype(BF16)
        o = jnp.dot(w, v, preferred_element_type=F32)
        o = jnp.where(out_pos < length, o, 0.0).astype(BF16)
        for g in range(heads):
            prefill_ref[i, :, g * HEAD : (g + 1) * HEAD] = o[g * share : (g + 1) * share]

    steps = step_out.shape[1] // heads
    qrows = heads * steps

    def step_arrival(j):
        source_req = t * per_dev + j
        return remote(
            msg_ref.at[0],
            step_in.at[j],
            step_send.at[0],
            step_got.at[j],
            req=source_req,
            tp=r // per_dev,
        )

    def out_copy(j, target):
        return remote(
            step_out.at[j],
            step_recv.at[r],
            out_send.at[j, target],
            out_got.at[r],
            req=t * per_dev + j,
            tp=target,
        )

    def out_arrival(source):
        return remote(
            step_out.at[0],
            step_recv.at[source],
            out_send.at[0, 0],
            out_got.at[source],
            req=source,
            tp=r // per_dev,
        )

    for j in range(per_dev):

        @pl.when(jnp.logical_not((t * per_dev + j == r) & (r // per_dev == t)))
        def _():
            step_arrival(j).wait_recv()

        n = 2 * j + p
        length = lens[t * prompts + n]
        k, v = k_full[n], v_full[n]
        got = step_in[j]
        qs = got[:qrows]
        tail = got[qrows:].astype(F32)
        new_k = tail[:SLOTS].astype(BF16)
        new_v = tail[SLOTS : 2 * SLOTS].astype(BF16)
        s_old = lax.dot_general(qs, k, (((1,), (1,)), ((), ())), preferred_element_type=F32) * scale
        s_new = (
            lax.dot_general(qs, new_k, (((1,), (1,)), ((), ())), preferred_element_type=F32) * scale
        )
        s_old = jnp.where(lax.broadcasted_iota(jnp.int32, (qrows, slots), 1) < length, s_old, NEG)
        at_step = lax.broadcasted_iota(jnp.int32, (qrows, SLOTS), 0) % steps
        at_new = lax.broadcasted_iota(jnp.int32, (qrows, SLOTS), 1)
        s_new = jnp.where(at_new <= at_step, s_new, NEG)
        top = jnp.maximum(
            jnp.max(s_old, axis=1, keepdims=True), jnp.max(s_new, axis=1, keepdims=True)
        )
        e_old, e_new = jnp.exp(s_old - top), jnp.exp(s_new - top)
        total = jnp.sum(e_old, axis=1, keepdims=True) + jnp.sum(e_new, axis=1, keepdims=True)
        mixed = jnp.zeros((qrows, HEAD), F32)
        for e, values in ((e_old, v), (e_new, new_v)):
            coarse = e.astype(BF16)
            fine = (e - coarse.astype(F32)).astype(BF16)
            mixed = mixed + jnp.dot(coarse, values, preferred_element_type=F32)
            mixed = mixed + jnp.dot(fine, values, preferred_element_type=F32)
        step_out[j] = (mixed / total).astype(BF16)
        for o in range(tp_count):
            target = (t + o) % tp_count
            if o == 0:

                @pl.when(t * per_dev + j == r)
                def _():
                    step_recv[r] = step_out[j]

                @pl.when(t * per_dev + j != r)
                def _():
                    out_copy(j, t).start()
            else:
                out_copy(j, target).start()

    for b in range(1, 2 * ring):
        hop(b, x_hbm, above).wait_send()
    for zz in range(ring):
        q_copy(zz).wait_send()
        side_copy(zz).wait_send()
        kv_copy(zz).wait_send()
    others(lambda target: low_copy(target).wait_send())
    others(lambda target: rank_copy(target, r).wait_send())
    uv_copy.wait_send()
    for i in range(per_dev):

        @pl.when(jnp.logical_not(step_self(i)))
        def _():
            step_copy(i).wait_send()

    for j in range(per_dev):
        for target in range(tp_count):

            @pl.when(jnp.logical_not((t * per_dev + j == r) & (target == t)))
            def _():
                out_copy(j, target).wait_send()

    def arrive(source, _):
        @pl.when(jnp.logical_not((source == r) & (r // per_dev == t)))
        def _():
            out_arrival(source).wait_recv()

        return 0

    lax.fori_loop(0, req_count, arrive, 0)
    decoded_ref[...] = step_recv[...]


def local(
    prompt_states,
    prompt_lengths,
    adapter_ids,
    w_query,
    w_key,
    value_weight,
    down_query,
    up_query,
    down_value,
    value_up_weight,
    step_queries,
    step_keyvals,
):
    req_count, tp_count = lax.axis_size("req"), lax.axis_size("tp")
    t = lax.axis_index("tp")
    prompts, slots, width = prompt_states.shape
    rows = prompts * slots
    cols = w_query.shape[1]
    kv_cols = w_key.shape[1]
    rank = down_query.shape[2]
    adapter_count = up_query.shape[0]
    ring = req_count // 2
    heads = cols // HEAD
    steps = step_queries.shape[1]
    per_dev = req_count // tp_count
    total_slots = req_count * slots

    qs = lax.dynamic_slice_in_dim(step_queries[0], t * per_dev * cols, per_dev * cols, 1)
    qs = qs.reshape(steps, per_dev, heads, HEAD).transpose(1, 2, 0, 3)
    qs = qs.reshape(per_dev, heads * steps, HEAD)
    kv = lax.dynamic_slice_in_dim(
        step_keyvals[0], t * per_dev * kv_cols, per_dev * kv_cols, 2
    ).reshape(steps, 2, per_dev // 2, HEAD)
    kv = jnp.repeat(kv.transpose(2, 1, 0, 3), 2, axis=0)
    kv = jnp.pad(kv, ((0, 0), (0, 0), (0, SLOTS - steps), (0, 0))).reshape(per_dev, 2 * SLOTS, HEAD)
    message = jnp.concatenate([qs, kv], axis=1)

    vmem = pl.BlockSpec(memory_space=pltpu.VMEM)
    smem = pl.BlockSpec(memory_space=pltpu.SMEM)
    hbm = pl.BlockSpec(memory_space=pl.ANY)
    dma = pltpu.SemaphoreType.DMA
    prefill, decoded = pl.pallas_call(
        functools.partial(kernel, req_count, tp_count),
        out_shape=(
            jax.ShapeDtypeStruct((prompts, total_slots // 2, cols), BF16),
            jax.ShapeDtypeStruct((req_count, heads * steps, HEAD), BF16),
        ),
        in_specs=[smem, smem] + [hbm] * 8 + [vmem],
        out_specs=(vmem, vmem),
        scratch_shapes=[
            pltpu.VMEM((req_count * rows, width), BF16),
            pltpu.VMEM((width, cols), BF16),
            pltpu.VMEM((SIDE, width), BF16),
            pltpu.VMEM((adapter_count, rank, cols), BF16),
            pltpu.VMEM((adapter_count, rank, kv_cols), BF16),
            pltpu.VMEM((2, ring, rows, cols), F32),
            pltpu.VMEM((ring, rows, cols), F32),
            pltpu.VMEM((2, ring, rows, SIDE), F32),
            pltpu.VMEM((2, ring, rows, SIDE), F32),
            pltpu.VMEM((2, ring, rows, HEAD), F32),
            pltpu.VMEM((2, ring, rows, HEAD), BF16),
            pltpu.VMEM((2, ring, rows, HEAD), BF16),
            pltpu.VMEM((req_count, rows, HEAD), BF16),
            pltpu.VMEM((req_count, rows, HEAD), BF16),
            pltpu.VMEM((req_count, rows, HEAD), BF16),
            pltpu.VMEM((prompts, rank, kv_cols), BF16),
            pltpu.VMEM((prompts, rank, kv_cols), BF16),
            pltpu.VMEM((prompts, total_slots, HEAD), BF16),
            pltpu.VMEM((prompts, total_slots, HEAD), BF16),
            pltpu.VMEM((per_dev, heads * steps + 2 * SLOTS, HEAD), BF16),
            pltpu.VMEM((per_dev, heads * steps, HEAD), BF16),
            pltpu.VMEM((req_count, heads * steps, HEAD), BF16),
            dma((8,)),
            dma((req_count,)),
            dma((req_count,)),
            dma((ring,)),
            dma((ring,)),
            dma((ring,)),
            dma((ring,)),
            dma((ring,)),
            dma((ring,)),
            dma((req_count,)),
            dma((req_count,)),
            dma((req_count,)),
            dma((req_count,)),
            dma((2,)),
            dma((per_dev,)),
            dma((per_dev,)),
            dma((per_dev, tp_count)),
            dma((req_count,)),
        ],
        compiler_params=pltpu.CompilerParams(
            collective_id=0, has_side_effects=True, vmem_limit_bytes=56 * 1024 * 1024
        ),
        cost_estimate=pl.CostEstimate(
            flops=2 * req_count * rows * width * (cols + SIDE),
            bytes_accessed=2 * width * (cols + SIDE),
            transcendentals=0,
        ),
    )(
        prompt_lengths,
        adapter_ids,
        prompt_states.reshape(rows, width),
        w_query,
        w_key.T,
        value_weight.T,
        down_query[0].T,
        down_value[0].T,
        up_query,
        value_up_weight,
        message,
    )
    decoded = decoded.reshape(req_count, heads, steps, HEAD).transpose(2, 0, 1, 3)
    return prefill, decoded.reshape(1, steps, req_count * cols)


def solution(mesh):
    in_specs = (
        P("tp", "req", "pp"),
        P(),
        P(),
        P("pp", "req"),
        P("pp", "req"),
        P("pp", "req"),
        P("req", "pp", None),
        P(None, None, "req"),
        P("req", "pp", None),
        P(None, None, "req"),
        P(("req", "pp"), None, None),
        P(("req", "pp"), None, None, None),
    )
    out_specs = (P("tp", "pp", "req"), P(("req", "pp"), None, None))
    return jax.shard_map(local, mesh=mesh, in_specs=in_specs, out_specs=out_specs, check_vma=False)
```

time: 456 us -> 91.4 us (0.20)
  waiting for transfers between devices: 346 us -> 0 us
  Pallas kernels: 0 us -> 85.9 us
  blocking collectives: 35.5 us -> 0 us
  matrix products: 17.2 us -> 0 us
  local copies, waits for them, and re-layouts: 20.8 us -> 4 us
  starting transfers between devices: 15.9 us -> 0 us
  between operations: 14.2 us -> 0.66 us
  other arithmetic: 5.67 us -> 0.61 us
    all_gather x4 -> x0, waiting for transfers between devices: 284 us -> none  [the longest x1 98.9 us: local(): piece = lax.all_gather(prompt_states, 'req', axis=1, tiled=True)]
    pallas_call x0 -> x1, Pallas kernels: none -> 85.9 us  [local(): pl.pallas_call(functools.partial(kernel, req_count, tp_count), out_shape=...]
    psum x1 -> x0, waiting for transfers between devices: 46.1 us -> none  [local(): query_sum, kv_sum, low_sum = lax.psum((query_part, kv_part, low_part), 'pp')]
    all_gather x2 -> x0, blocking collectives: 28.7 us -> none  [joined(): pieces = jax.tree.map(lambda part: lax.all_gather(part, axis), value)]
    dot_general x13 -> x0, matrix products: 17.2 us -> none  [the longest x1 3.84 us: local(): base_key = jnp.dot(flat, w_key, preferred_element_type=single_float)]
    all_to_all x2 -> x0, starting transfers between devices: 14.2 us -> none  [the longest x1 9.28 us: local(): lax.all_to_all(lax.all_to_all(own_slots, 'tp', split_axis=1, concat_axis=...]
    all_to_all x2 -> x0, waiting for transfers between devices: 12.6 us -> none  [the longest x1 8.47 us: local(): lax.all_to_all(lax.all_to_all(own_slots, 'tp', split_axis=1, concat_axis=...]
    gather x4 -> x0, local copies, waits for them, and re-layouts: 7.62 us -> none  [the longest x1 2.8 us: local(): rank_value = jnp.take(table_value, my_adapters, axis=0)]
  transfers between devices with their start and end apart: 9 -> 0, of which waited for: 8 -> 0; matrix products, arithmetic and copies ran while one was open for 6% -> 0% of each run, Pallas kernels for 0% -> 0%
where the time goes in v1:
time: 91.4 us; the launch traced here: 91.2 us
  Pallas kernels  85.9 us (94%)
  local copies, waits for them, and re-layouts  4 us (4%)
    pallas_call x1, Pallas kernels, local(): pl.pallas_call(functools.partial(kernel, req_count, tp_count), out_shape=...  85.9 us
    unnamed x4, local copies, waits for them, and re-layouts  3.25 us

profile of v1, /device:TPU:1, one launch (start us, length us, event | category | flops | bytes accessed | tf_op | source)
XLA Modules:
  0.0 91.2 jit_solution(16655363963324065293)
XLA Ops:
  0.6 0.0 copy-start
  0.7 0.7 dynamic-slice_bitcast_fusion
  1.4 0.1 copy-done
  1.5 0.6 pad_maximum_fusion.msg_ref
  2.1 85.9 %shard_map.131 = (bf16[4,64,512]{2,1,0:T(8,128)(2,1)}, bf16[16,16,128]{2,1,0:T(8,128)(2,1)}) custom-call(s32[32]{0:T(128)} %lens.1, s32[32]{0:T(128)} %adapters.1, bf16[32,4096]{1,0:T(8,128)(2,1)} %bitcast.33, bf16[4096,512]{1,0:T(8,128)(2,1)} %wq_hbm.1, bf16[64,4096]{1,0:T(8,128)(2,1)} %bitcast.31, bf16[64,4096]{1,0:T(8,128)(2,1)} %bitcast.32, ...), custom_call_target="tpu_custom_call" | custom-call | flops 3221225472 | bytes 6291456 | tf_op jit(solution)/shard_map/pallas_call | solution.py:546
  88.0 1.7 %copy.22 = bf16[4,64,512]{2,1,0:T(8,128)(2,1)} copy(bf16[4,64,512]{2,1,0:T(8,128)(2,1)} %get-tuple-element.8) | data formatting | bytes 524288
  89.7 1.5 %copy.23 = bf16[1,4,8192]{2,1,0:T(4,128)(2,1)} copy(bf16[1,4,8192]{2,1,0:T(4,128)(2,1)} %bitcast.28) | data formatting | bytes 131072
  (4 shorter events, 0.0 us)
Async XLA Ops:
  0.6 0.8 copy-start

commit v2 on v1

--- a/solution.py
+++ b/solution.py
@@ -37,9 +37,11 @@
     side_w,
     uq,
     uv,
-    qbuf,
+    q_keep,
+    q_out,
     qrecv,
     side,
+    side_out,
     siderecv,
     kv_own,
     kvsend,
@@ -47,6 +49,9 @@
     lowsend,
     lowrecv,
     rank_all,
+    late_out,
+    late_in,
+    ranks_f32,
     uv_send,
     uv_recv,
     k_full,
@@ -67,6 +72,8 @@
     low_recv,
     rank_send,
     rank_recv,
+    late_send,
+    late_recv,
     uv_sems,
     step_send,
     step_got,
@@ -78,7 +85,8 @@
     h, z = r // ring, r % ring
     rows = x_hbm.shape[0]
     prompts = rows // SLOTS
-    cols = qbuf.shape[3]
+    cols = q_keep.shape[2]
+    part = rows // 2
     heads = cols // HEAD
     per_dev = msg_ref.shape[0]
     above = h * ring + (z + 1) % ring
@@ -128,19 +136,26 @@
         )
     pl.semaphore_wait(barrier, 3 + tp_count)
 
-    def block(b):
-        return blocks.at[pl.ds(pl.multiple_of(b * rows, rows), rows)]
-
-    def hop(b, src, req):
-        return remote(src, block(b), ring_send.at[b], ring_recv.at[b], req=req)
+    def piece(b, s):
+        return blocks.at[pl.ds(pl.multiple_of(b * rows + s * part, part), part)]
+
+    def own_piece(s):
+        return x_hbm.at[pl.ds(s * part, part)]
+
+    def hop(b, s, src, req):
+        return remote(src, piece(b, s), ring_send.at[b, s], ring_recv.at[b, s], req=req)
+
+    def arrive_hop(b, s):
+        hop(b, s, own_piece(s), across).wait_recv()
 
     half = ring // 2
     last = 2 * ring - 2
 
-    hop(1, x_hbm, across).start()
-    hop(2, x_hbm, above).start()
-    if half > 1:
-        hop(3, x_hbm, below).start()
+    for s in range(2):
+        hop(2, s, own_piece(s), above).start()
+        if half > 1:
+            hop(3, s, own_piece(s), below).start()
+        hop(1, s, own_piece(s), across).start()
 
     kv_cols, rank = wk_hbm.shape[0], dq_hbm.shape[0]
     used = 2 * kv_cols + 2 * rank
@@ -150,24 +165,32 @@
 
     def project(c, places):
         a = blocks[pl.ds(pl.multiple_of(c * 2 * rows, 2 * rows), 2 * rows), :]
+        got = lax.dot_general(
+            a, side_w[...], (((1,), (1,)), ((), ())), preferred_element_type=F32
+        )
+        for i, (zz, hh) in enumerate(places):
+            side[hh, zz] = got[i * rows : (i + 1) * rows]
+            side_out[hh, zz] = got[i * rows : (i + 1) * rows].astype(BF16)
         for n in range(0, cols, 256):
             width = min(256, cols - n)
             got = jnp.dot(a, weights[:, n : n + width], preferred_element_type=F32)
             for i, (zz, hh) in enumerate(places):
-                sent = jnp.where(hh == p, 0, 1)
-                qbuf[sent, zz, :, n : n + width] = got[i * rows : (i + 1) * rows]
-        got = lax.dot_general(
-            a, side_w[...], (((1,), (1,)), ((), ())), preferred_element_type=F32
-        )
-        for i, (zz, hh) in enumerate(places):
-            side[hh, zz] = got[i * rows : (i + 1) * rows]
+                mine = got[i * rows : (i + 1) * rows]
+
+                @pl.when(hh == p)
+                def _():
+                    q_keep[zz, :, n : n + width] = mine
+
+                @pl.when(hh != p)
+                def _():
+                    q_out[zz, :, n : n + width] = mine.astype(BF16)
 
     def q_copy(zz):
-        return remote(qbuf.at[1, zz], qrecv.at[zz], q_send.at[zz], q_recv.at[zz], pp=other)
+        return remote(q_out.at[zz], qrecv.at[zz], q_send.at[zz], q_recv.at[zz], pp=other)
 
     def side_copy(zz):
         return remote(
-            side.at[:, zz], siderecv.at[:, zz], side_send.at[zz], side_recv.at[zz], pp=other
+            side_out.at[:, zz], siderecv.at[:, zz], side_send.at[zz], side_recv.at[zz], pp=other
         )
 
     def exchange(zz):
@@ -189,6 +212,7 @@
             lowsend.at[source], lowrecv.at[source], low_send.at[source], low_recv.at[source], req=source
         )
 
+    near_lane = lax.broadcasted_iota(jnp.int32, (rows, HEAD), 1) < HEAD // 2
     prompt_of = lax.broadcasted_iota(jnp.int32, (rows, HEAD), 0) // SLOTS
     match = jnp.zeros((rows, HEAD), F32)
     for i in range(prompts):
@@ -198,7 +222,7 @@
     def finish(zz, self_too):
         side_copy(zz).wait_recv()
         for hh in range(2):
-            total = side[hh, zz] + siderecv[hh, zz]
+            total = side[hh, zz] + siderecv[hh, zz].astype(F32)
             kv_own[hh, zz] = total[:, :HEAD]
             kvsend[hh, zz] = total[:, :HEAD].astype(BF16)
             low = jnp.where(match > 0.0, total[:, HEAD:SIDE], 0.0).astype(BF16)
@@ -217,44 +241,50 @@
                 low_copy(target).start()
         kv_copy(zz).start()
 
-    hop(1, x_hbm, across).wait_recv()
-    if half > 1:
-        hop(4, block(1), above).start()
-        hop(5, block(1), below).start()
-    else:
-        hop(3, block(1), below).start()
-
+    def ahead(k):
+        return (z + ring - k) % ring, (z + k) % ring
+
+    for s in range(2):
+        if half > 1:
+            arrive_hop(2, s)
+            if half > 2:
+                hop(6, s, piece(2, s), above).start()
+            hop(4, s, piece(2, s), across).start()
+            arrive_hop(3, s)
+            if half > 2:
+                hop(7, s, piece(3, s), below).start()
+            hop(5, s, piece(3, s), across).start()
+    for s in range(2):
+        arrive_hop(1, s)
+        if half == 1:
+            hop(3, s, piece(1, s), below).start()
     project(0, [(z, h), (z, 1 - h)])
     exchange(z)
+    if half > 1:
+        up, down = ahead(1)
+        project(1, [(up, h), (down, h)])
 
     def step(k, _):
         base = 2 + 4 * (k - 1)
-        up, down = (z + ring - k) % ring, (z + k) % ring
-        hop(base, x_hbm, above).wait_recv()
-        hop(base + 4, block(base), above).start()
-        hop(base + 1, x_hbm, below).wait_recv()
-
-        @pl.when(k + 1 < half)
-        def _():
-            hop(base + 5, block(base + 1), below).start()
-
-        project(1 + 2 * (k - 1), [(up, h), (down, h)])
-        hop(base + 2, x_hbm, above).wait_recv()
-
-        @pl.when(k + 1 < half)
-        def _():
-            hop(base + 6, block(base + 2), above).start()
-
-        hop(base + 3, x_hbm, below).wait_recv()
-
-        @pl.when(k + 1 < half)
-        def _():
-            hop(base + 7, block(base + 3), below).start()
-
-        @pl.when(k + 1 == half)
-        def _():
-            hop(last + 1, block(base + 3), below).start()
-
+        for s in range(2):
+            for side_of in range(2):
+                arrive_hop(base + 4 + side_of, s)
+
+                @pl.when(k + 2 < half)
+                def _():
+                    hop(
+                        base + 8 + side_of, s, piece(base + 4 + side_of, s), (above, below)[side_of]
+                    ).start()
+
+        up, down = ahead(k + 1)
+        project(1 + 2 * k, [(up, h), (down, h)])
+        for s in range(2):
+            for side_of in range(2):
+                arrive_hop(base + 2 + side_of, s)
+                hop(
+                    base + 6 + side_of, s, piece(base + 2 + side_of, s), (above, below)[side_of]
+                ).start()
+        up, down = ahead(k)
         project(2 + 2 * (k - 1), [(up, 1 - h), (down, 1 - h)])
         exchange(up)
         exchange(down)
@@ -265,20 +295,36 @@
 
         @pl.when(k > 1)
         def _():
-            finish((z + ring - k + 1) % ring, False)
-            finish((z + k - 1) % ring, False)
+            for zz in ahead(k - 1):
+                finish(zz, False)
 
         return 0
 
-    lax.fori_loop(1, half, step, 0)
+    lax.fori_loop(1, half - 1, step, 0)
+    if half > 1:
+        base = 2 + 4 * (half - 2)
+        for s in range(2):
+            arrive_hop(base + 2, s)
+            hop(last, s, piece(base, s), above).start()
+            arrive_hop(base + 3, s)
+            hop(last + 1, s, piece(base + 3, s), below).start()
+        up, down = ahead(half - 1)
+        project(2 + 2 * (half - 2), [(up, 1 - h), (down, 1 - h)])
+        exchange(up)
+        exchange(down)
+        if half == 2:
+            finish(z, True)
+        else:
+            for zz in ahead(half - 2):
+                finish(zz, False)
+        for zz in ahead(half - 1):
+            finish(zz, False)
+    else:
+        finish(z, True)
     far = (z + half) % ring
-    if half == 1:
-        finish(z, True)
-    else:
-        finish((z + ring - half + 1) % ring, False)
-        finish((z + half - 1) % ring, False)
-    hop(last, x_hbm, above).wait_recv()
-    hop(last + 1, x_hbm, below).wait_recv()
+    for s in range(2):
+        arrive_hop(last, s)
+        arrive_hop(last + 1, s)
     project(ring - 1, [(far, h), (far, 1 - h)])
     exchange(far)
 
@@ -311,7 +357,19 @@
     uv_copy = remote(uv_send, uv_recv, uv_sems.at[0], uv_sems.at[1], req=pair)
     uv_copy.start()
 
-    finish(far, False)
+    def near(body):
+        def one(o, _):
+            other_z = (z + o) % ring
+
+            @pl.when(other_z != far)
+            def _():
+                body(h * ring + other_z)
+                body((1 - h) * ring + other_z)
+
+            return 0
+
+        body((1 - h) * ring + z)
+        lax.fori_loop(1, ring, one, 0)
 
     def others(body):
         def one(o, _):
@@ -320,7 +378,9 @@
 
         lax.fori_loop(1, req_count, one, 0)
 
-    others(lambda source: low_arrival(source).wait_recv())
+    near(lambda source: low_arrival(source).wait_recv())
+    for hh in range(2):
+        lowrecv[hh * ring + far] = jnp.zeros((rows, HEAD), BF16)
     low = lowrecv[0].astype(F32)
     for source in range(1, req_count):
         low = low + lowrecv[source].astype(F32)
@@ -331,31 +391,49 @@
             rank_all.at[slot], rank_all.at[slot], rank_send.at[target], rank_recv.at[slot], req=target
         )
 
+    def late_copy(target, slot):
+        return remote(
+            late_out, late_in.at[slot], late_send.at[target], late_recv.at[slot], req=target
+        )
+
     others(lambda target: rank_copy(target, r).start())
+
+    side_copy(far).wait_recv()
+    late = []
+    for hh in range(2):
+        total = side[hh, far] + siderecv[hh, far].astype(F32)
+        kv_own[hh, far] = total[:, :HEAD]
+        kvsend[hh, far] = total[:, :HEAD].astype(BF16)
+        late.append(jnp.where(match > 0.0, total[:, HEAD:SIDE], 0.0))
+    packed = jnp.where(near_lane, late[0], pltpu.roll(late[1], HEAD // 2, 1)).astype(BF16)
+    late_out[...] = packed
+    late_in[r] = packed
+    others(lambda target: late_copy(target, r).start())
+    kv_copy(far).start()
 
     for zz in range(ring):
         kv_copy(zz).wait_recv()
-        q_copy(zz).wait_recv()
     uv_copy.wait_recv()
     others(lambda source: rank_copy(source, source).wait_recv())
+    others(lambda source: late_copy(source, source).wait_recv())
 
     even = r % 2 == 0
     slots = req_count * SLOTS
     share = slots // 2
     own = kv_own[...].reshape(req_count, prompts, SLOTS, HEAD)
     oth = kvrecv[...].astype(F32).reshape(req_count, prompts, SLOTS, HEAD)
-    ranks = rank_all[...].astype(F32).reshape(req_count, prompts, SLOTS, HEAD)
-    base_q = (qbuf[0] + qrecv[...]).reshape(ring, prompts, SLOTS, cols)
-    my_ranks = rank_all[pl.ds(p * ring, ring)].astype(F32).reshape(ring, prompts, SLOTS, HEAD)
+    for zz in range(ring):
+        sender = (zz + half) % ring
+        both = late_in[sender].astype(F32) + late_in[ring + sender].astype(F32)
+        ranks_f32[zz] = rank_all[zz].astype(F32) + jnp.where(near_lane, both, 0.0)
+        ranks_f32[ring + zz] = rank_all[ring + zz].astype(F32) + jnp.where(
+            near_lane, pltpu.roll(both, HEAD // 2, 1), 0.0
+        )
+    ranks = ranks_f32[...].reshape(req_count, prompts, SLOTS, HEAD)
     lane = lax.broadcasted_iota(jnp.int32, (slots, HEAD), 1)
     low_lane = lane < HEAD // 2
     scale = HEAD ** (-0.5)
-    row_pos = lax.broadcasted_iota(jnp.int32, (heads * share, slots), 0) % share + p * share
-    col_pos = lax.broadcasted_iota(jnp.int32, (heads * share, slots), 1)
-    out_pos = lax.broadcasted_iota(jnp.int32, (heads * share, HEAD), 0) % share + p * share
     for i in range(prompts):
-        length = lens[t * prompts + i]
-        adapter = adapters[t * prompts + i]
         mine = own[:, i].reshape(slots, HEAD)
         theirs = oth[:, i].reshape(slots, HEAD)
         first = jnp.where(even, mine, theirs)
@@ -368,23 +446,8 @@
         )
         rank_rows = ranks[:, i].reshape(slots, HEAD).astype(BF16)
         v = v_base + jnp.dot(rank_rows[:, rank : 2 * rank], up_v, preferred_element_type=F32)
-        v = v.astype(BF16)
         k_full[i] = k
-        v_full[i] = v
-        rank_q = my_ranks[:, i].reshape(share, HEAD).astype(BF16)[:, :rank]
-        q = base_q[:, i].reshape(share, cols) + jnp.dot(
-            rank_q, uq[adapter], preferred_element_type=F32
-        )
-        q = q.astype(BF16)
-        q = jnp.concatenate([q[:, g * HEAD : (g + 1) * HEAD] for g in range(heads)], axis=0)
-        s = lax.dot_general(q, k, (((1,), (1,)), ((), ())), preferred_element_type=F32) * scale
-        s = jnp.where((col_pos <= row_pos) & (col_pos < length), s, NEG)
-        e = jnp.exp(s - jnp.max(s, axis=1, keepdims=True))
-        w = (e / jnp.sum(e, axis=1, keepdims=True)).astype(BF16)
-        o = jnp.dot(w, v, preferred_element_type=F32)
-        o = jnp.where(out_pos < length, o, 0.0).astype(BF16)
-        for g in range(heads):
-            prefill_ref[i, :, g * HEAD : (g + 1) * HEAD] = o[g * share : (g + 1) * share]
+        v_full[i] = v.astype(BF16)
 
     steps = step_out.shape[1] // heads
     qrows = heads * steps
@@ -468,13 +531,41 @@
             else:
                 out_copy(j, target).start()
 
+    for zz in range(ring):
+        q_copy(zz).wait_recv()
+    base_q = (q_keep[...] + qrecv[...].astype(F32)).reshape(ring, prompts, SLOTS, cols)
+    my_ranks = ranks_f32[pl.ds(p * ring, ring)].reshape(ring, prompts, SLOTS, HEAD)
+    row_pos = lax.broadcasted_iota(jnp.int32, (heads * share, slots), 0) % share + p * share
+    col_pos = lax.broadcasted_iota(jnp.int32, (heads * share, slots), 1)
+    out_pos = lax.broadcasted_iota(jnp.int32, (heads * share, HEAD), 0) % share + p * share
+    for i in range(prompts):
+        length = lens[t * prompts + i]
+        adapter = adapters[t * prompts + i]
+        k, v = k_full[i], v_full[i]
+        rank_q = my_ranks[:, i].reshape(share, HEAD).astype(BF16)[:, :rank]
+        q = base_q[:, i].reshape(share, cols) + jnp.dot(
+            rank_q, uq[adapter], preferred_element_type=F32
+        )
+        q = q.astype(BF16)
+        q = jnp.concatenate([q[:, g * HEAD : (g + 1) * HEAD] for g in range(heads)], axis=0)
+        s = lax.dot_general(q, k, (((1,), (1,)), ((), ())), preferred_element_type=F32) * scale
+        s = jnp.where((col_pos <= row_pos) & (col_pos < length), s, NEG)
+        e = jnp.exp(s - jnp.max(s, axis=1, keepdims=True))
+        w = (e / jnp.sum(e, axis=1, keepdims=True)).astype(BF16)
+        o = jnp.dot(w, v, preferred_element_type=F32)
+        o = jnp.where(out_pos < length, o, 0.0).astype(BF16)
+        for g in range(heads):
+            prefill_ref[i, :, g * HEAD : (g + 1) * HEAD] = o[g * share : (g + 1) * share]
+
     for b in range(1, 2 * ring):
-        hop(b, x_hbm, above).wait_send()
+        for s in range(2):
+            hop(b, s, own_piece(s), above).wait_send()
     for zz in range(ring):
         q_copy(zz).wait_send()
         side_copy(zz).wait_send()
         kv_copy(zz).wait_send()
-    others(lambda target: low_copy(target).wait_send())
+    near(lambda target: low_copy(target).wait_send())
+    others(lambda target: late_copy(target, r).wait_send())
     others(lambda target: rank_copy(target, r).wait_send())
     uv_copy.wait_send()
     for i in range(per_dev):
@@ -557,16 +648,21 @@
             pltpu.VMEM((SIDE, width), BF16),
             pltpu.VMEM((adapter_count, rank, cols), BF16),
             pltpu.VMEM((adapter_count, rank, kv_cols), BF16),
-            pltpu.VMEM((2, ring, rows, cols), F32),
             pltpu.VMEM((ring, rows, cols), F32),
+            pltpu.VMEM((ring, rows, cols), BF16),
+            pltpu.VMEM((ring, rows, cols), BF16),
             pltpu.VMEM((2, ring, rows, SIDE), F32),
-            pltpu.VMEM((2, ring, rows, SIDE), F32),
+            pltpu.VMEM((2, ring, rows, SIDE), BF16),
+            pltpu.VMEM((2, ring, rows, SIDE), BF16),
             pltpu.VMEM((2, ring, rows, HEAD), F32),
             pltpu.VMEM((2, ring, rows, HEAD), BF16),
             pltpu.VMEM((2, ring, rows, HEAD), BF16),
             pltpu.VMEM((req_count, rows, HEAD), BF16),
             pltpu.VMEM((req_count, rows, HEAD), BF16),
             pltpu.VMEM((req_count, rows, HEAD), BF16),
+            pltpu.VMEM((rows, HEAD), BF16),
+            pltpu.VMEM((req_count, rows, HEAD), BF16),
+            pltpu.VMEM((req_count, rows, HEAD), F32),
             pltpu.VMEM((prompts, rank, kv_cols), BF16),
             pltpu.VMEM((prompts, rank, kv_cols), BF16),
             pltpu.VMEM((prompts, total_slots, HEAD), BF16),
@@ -575,14 +671,16 @@
             pltpu.VMEM((per_dev, heads * steps, HEAD), BF16),
             pltpu.VMEM((req_count, heads * steps, HEAD), BF16),
             dma((8,)),
-            dma((req_count,)),
-            dma((req_count,)),
+            dma((req_count, 2)),
+            dma((req_count, 2)),
             dma((ring,)),
             dma((ring,)),
             dma((ring,)),
             dma((ring,)),
             dma((ring,)),
             dma((ring,)),
+            dma((req_count,)),
+            dma((req_count,)),
             dma((req_count,)),
             dma((req_count,)),
             dma((req_count,)),

time: 91.4 us -> 78.5 us (0.86)
  Pallas kernels: 85.9 us -> 72.9 us
    pallas_call x1, Pallas kernels: 85.9 us -> 72.9 us  [local(): pl.pallas_call(functools.partial(kernel, req_count, tp_count), out_shape=...]
where the time goes in v2:
time: 78.5 us; the launch traced here: 78.2 us
  Pallas kernels  72.9 us (93%)
  local copies, waits for them, and re-layouts  4 us (5%)
    pallas_call x1, Pallas kernels, local(): pl.pallas_call(functools.partial(kernel, req_count, tp_count), out_shape=...  72.9 us
    unnamed x4, local copies, waits for them, and re-layouts  3.25 us

profile of v2, /device:TPU:1, one launch (start us, length us, event | category | flops | bytes accessed | tf_op | source)
XLA Modules:
  0.0 78.2 jit_solution(17278907268823649915)
XLA Ops:
  0.6 0.0 copy-start
  0.7 0.7 dynamic-slice_bitcast_fusion
  1.4 0.1 copy-done
  1.5 0.6 pad_maximum_fusion.msg_ref
  2.1 72.9 %shard_map.131 = (bf16[4,64,512]{2,1,0:T(8,128)(2,1)}, bf16[16,16,128]{2,1,0:T(8,128)(2,1)}) custom-call(s32[32]{0:T(128)} %lens.1, s32[32]{0:T(128)} %adapters.1, bf16[32,4096]{1,0:T(8,128)(2,1)} %bitcast.33, bf16[4096,512]{1,0:T(8,128)(2,1)} %wq_hbm.1, bf16[64,4096]{1,0:T(8,128)(2,1)} %bitcast.31, bf16[64,4096]{1,0:T(8,128)(2,1)} %bitcast.32, ...), custom_call_target="tpu_custom_call" | custom-call | flops 3221225472 | bytes 6291456 | tf_op jit(solution)/shard_map/pallas_call | solution.py:637
  75.0 1.7 %copy.22 = bf16[4,64,512]{2,1,0:T(8,128)(2,1)} copy(bf16[4,64,512]{2,1,0:T(8,128)(2,1)} %get-tuple-element.8) | data formatting | bytes 524288
  76.7 1.5 %copy.23 = bf16[1,4,8192]{2,1,0:T(4,128)(2,1)} copy(bf16[1,4,8192]{2,1,0:T(4,128)(2,1)} %bitcast.28) | data formatting | bytes 131072
  (4 shorter events, 0.0 us)
Async XLA Ops:
  0.6 0.8 %copy-start = (bf16[1,4,8192]{2,1,0:T(4,128)(2,1)S(1)}, bf16[1,4,8192]{2,1,0:T(4,128)(2,1)}, u32[]{:S(2)}) copy-start(bf16[1,4,8192]{2,1,0:T(4,128)(2,1)} %param.22) | copy-start | bytes 196612

commit v3 on v1

v3 whole, which is shorter than its diff:
```python
import functools

import jax
import jax.numpy as jnp
from jax import lax
from jax.experimental import pallas as pl
from jax.experimental.pallas import tpu as pltpu
from jax.sharding import PartitionSpec as P

HEAD = 128
SLOTS = 8
SIDE = 256
NEG = -1e30
F32 = jnp.float32
BF16 = jnp.bfloat16
MESH = pl.DeviceIdType.MESH


def kernel(
    req_count,
    tp_count,
    lens,
    adapters,
    x_hbm,
    wq_hbm,
    wk_hbm,
    wv_hbm,
    dq_hbm,
    dv_hbm,
    uq_hbm,
    uv_hbm,
    msg_ref,
    prefill_ref,
    decoded_ref,
    blocks,
    weights,
    side_w,
    uq,
    uv,
    q_keep,
    q_out,
    q_in,
    a_own,
    a_out,
    a_in,
    b_own,
    b_out,
    b_in,
    kv_own,
    kv_oth,
    kv_out,
    kv_in,
    late_in,
    low_out,
    low_in,
    rank_all,
    ranks,
    uv_out,
    uv_in,
    k_full,
    v_full,
    step_in,
    step_out,
    step_recv,
    load_sem,
    ring_send,
    ring_recv,
    map_send,
    map_recv,
    q_send,
    q_recv,
    a_send,
    a_recv,
    b_send,
    b_recv,
    kv_send,
    kv_recv,
    late_send,
    late_recv,
    low_send,
    low_recv,
    rank_send,
    rank_recv,
    uv_sems,
    step_send,
    step_got,
    out_send,
    out_got,
):
    r, t, p = lax.axis_index("req"), lax.axis_index("tp"), lax.axis_index("pp")
    ring = req_count // 2
    half = ring // 2
    h, z = r // ring, r % ring
    rows = x_hbm.shape[0]
    part = rows // 2
    prompts = rows // SLOTS
    cols = q_keep.shape[2]
    heads = cols // HEAD
    per_dev = msg_ref.shape[0]
    kv_cols, rank = wk_hbm.shape[0], dq_hbm.shape[0]
    maps = 2 * rank
    above = h * ring + (z + 1) % ring
    below = h * ring + (z + ring - 1) % ring
    across = (1 - h) * ring + z
    other = 1 - p
    pair = r + 1 - 2 * (r % 2)
    far = (z + half) % ring
    pair_far = (pair % ring + half) % ring

    def remote(src, dst, send, recv, req=None, tp=None, pp=None):
        where = (r if req is None else req, t if tp is None else tp, p if pp is None else pp)
        return pltpu.make_async_remote_copy(
            src_ref=src,
            dst_ref=dst,
            send_sem=send,
            recv_sem=recv,
            device_id=where,
            device_id_type=MESH,
        )

    loads = [
        pltpu.make_async_copy(src, dst, load_sem.at[i])
        for i, (src, dst) in enumerate(
            [
                (dq_hbm, side_w.at[pl.ds(2 * kv_cols, rank)]),
                (dv_hbm, side_w.at[pl.ds(2 * kv_cols + rank, rank)]),
                (wk_hbm, side_w.at[pl.ds(0, kv_cols)]),
                (wv_hbm, side_w.at[pl.ds(kv_cols, kv_cols)]),
                (x_hbm, blocks.at[pl.ds(0, rows)]),
                (wq_hbm, weights),
                (uq_hbm, uq),
                (uv_hbm, uv),
            ]
        )
    ]
    for load in loads:
        load.start()

    barrier = pltpu.get_barrier_semaphore()
    for where in ((above, t, p), (below, t, p), (across, t, p), (r, t, other)):
        pl.semaphore_signal(barrier, inc=1, device_id=where, device_id_type=MESH)
    for o in range(1, tp_count):
        pl.semaphore_signal(
            barrier, inc=1, device_id=(r, (t + o) % tp_count, p), device_id_type=MESH
        )
    pl.semaphore_wait(barrier, 3 + tp_count)

    def own(k, way=0):
        return 0 if k == 0 else 2 + 4 * (k - 1) + (way if k < half else -2)

    def cross(k, way=0):
        if k == 0:
            return 1
        if k == half:
            return 2 * ring - 1
        return 2 + 4 * (k - 1) + (2 if k < half - 1 else 3) + way

    def piece(b, s):
        return blocks.at[pl.ds(b * rows + s * part, part)]

    def own_piece(s):
        return x_hbm.at[pl.ds(s * part, part)]

    def hop(b, s, src, req):
        return remote(src, piece(b, s), ring_send.at[b, s], ring_recv.at[b, s], req=req)

    def arrive(b, s):
        hop(b, s, own_piece(s), across).wait_recv()

    toward = (above, below)
    order = ((0, 0), (1, 1), (0, 1), (1, 0))

    for way, s in order:
        hop(own(1, way), s, own_piece(s), toward[way]).start()

    strip = side_w.shape[1] // tp_count

    def map_at(first, owner):
        return side_w.at[
            pl.ds(first, maps), pl.ds(pl.multiple_of(owner * strip, strip), strip)
        ]

    map_row = 2 * kv_cols + maps

    def map_hop():
        return remote(
            map_at(2 * kv_cols, t), map_at(map_row, t), map_send.at[t], map_recv.at[t], req=across
        )

    def map_spread(target, owner):
        return remote(
            map_at(map_row, owner),
            map_at(map_row, owner),
            map_send.at[target],
            map_recv.at[owner],
            tp=target,
        )

    for load in loads[:2]:
        load.wait()
    map_hop().start()
    for s in range(2):
        hop(cross(0), s, own_piece(s), across).start()
    for load in loads[2:]:
        load.wait()
    map_hop().wait_recv()
    for o in range(1, tp_count):
        map_spread((t + o) % tp_count, t).start()

    def q_copy(zz):
        return remote(q_out.at[zz], q_in.at[zz], q_send.at[zz], q_recv.at[zz], pp=other)

    def a_copy(zz):
        return remote(a_out.at[zz], a_in.at[zz], a_send.at[zz], a_recv.at[zz], pp=other)

    def b_copy(zz):
        return remote(b_out.at[zz], b_in.at[zz], b_send.at[zz], b_recv.at[zz], pp=other)

    def late_copy(i):
        return remote(
            b_out.at[far],
            late_in.at[i],
            late_send.at[i],
            late_recv.at[i],
            req=pair,
            pp=(p, other)[i],
        )

    def project(first, places, in_own, late=False):
        count = len(places) * rows
        at = pl.ds(first * rows, count)
        side = SIDE if any(in_own) else HEAD
        got = lax.dot_general(
            blocks[at, :],
            side_w[:side],
            (((1,), (1,)), ((), ())),
            preferred_element_type=F32,
        )
        for i, (zz, mine) in enumerate(zip(places, in_own)):
            block = got[i * rows : (i + 1) * rows]
            if mine:
                a_own[zz] = block
                a_out[zz] = block.astype(BF16)
                a_copy(zz).start()
            else:
                b_own[zz] = block[:, :HEAD]
                b_out[zz] = block[:, :HEAD].astype(BF16)
                b_copy(zz).start()
                if late:
                    late_copy(0).start()
                    late_copy(1).start()

        def part_of(n, _):
            lanes = pl.ds(pl.multiple_of(n * SIDE, SIDE), SIDE)
            got = jnp.dot(blocks[at, :], weights[:, lanes], preferred_element_type=F32)
            for i, (zz, mine) in enumerate(zip(places, in_own)):
                block = got[i * rows : (i + 1) * rows]
                keep = (h == p) if mine else (h != p)

                @pl.when(keep)
                def _():
                    q_keep[zz, :, lanes] = block

                @pl.when(jnp.logical_not(keep))
                def _():
                    q_out[zz, :, lanes] = block.astype(BF16)

            return 0

        lax.fori_loop(0, cols // SIDE, part_of, 0)
        for zz, mine in zip(places, in_own):

            @pl.when((h != p) if mine else (h == p))
            def _():
                q_copy(zz).start()

    def kv_copy(hh, zz):
        return remote(
            kv_out.at[hh, zz],
            kv_in.at[hh, zz],
            kv_send.at[hh, zz],
            kv_recv.at[hh, zz],
            req=pair,
        )

    def low_copy(zz):
        return remote(
            low_out.at[zz], low_in.at[z], low_send.at[zz], low_recv.at[z], req=h * ring + zz
        )

    def low_arrival(zz):
        return remote(
            low_out.at[zz], low_in.at[zz], low_send.at[zz], low_recv.at[zz], req=h * ring + zz
        )

    near_lane = lax.broadcasted_iota(jnp.int32, (rows, HEAD), 1) < maps
    prompt_of = lax.broadcasted_iota(jnp.int32, (rows, HEAD), 0) // SLOTS
    match = jnp.zeros((rows, HEAD), F32)
    for i in range(prompts):
        adapter = adapters[t * prompts + i]
        mine = jnp.where(adapter == r, 1.0, 0.0)
        theirs = jnp.where(adapter == across, 1.0, 0.0)
        match = jnp.where(prompt_of == i, jnp.where(near_lane, mine, theirs), match)

    def finish_kv(hh, zz, total):
        kv_own[hh, zz] = total
        kv_out[hh, zz] = total.astype(BF16)
        kv_copy(hh, zz).start()

    def finish_own(zz, self_too=False):
        a_copy(zz).wait_recv()
        total = a_own[zz] + a_in[zz].astype(F32)
        finish_kv(h, zz, total[:, :HEAD])
        low = jnp.where(match > 0.0, total[:, HEAD:SIDE], 0.0)
        low = low + pltpu.roll(low, HEAD // 2, 1)
        packed = jnp.where(near_lane[:part], low[:part], low[part:]).astype(BF16)
        if self_too:
            low_in[zz] = packed
        else:
            low_out[zz] = packed
            low_copy(zz).start()

    def finish_cross(zz):
        b_copy(zz).wait_recv()
        finish_kv(1 - h, zz, b_own[zz] + b_in[zz].astype(F32))

    def ahead(k):
        return [(z + ring - k) % ring, (z + k) % ring]

    def arrive_own(k):
        for way, s in order:
            arrive(own(k, way), s)
            src = piece(own(k, way), s)
            if k < half - 1:
                hop(own(k + 1, way), s, src, toward[way]).start()
            elif s == way:
                hop(own(half), s, src, toward[way]).start()
            if k == 1:
                hop(cross(1, way), s, src, across).start()

    def arrive_cross(k):
        for way, s in order:
            arrive(cross(k, way), s)
            src = piece(cross(k, way), s)
            if k < half - 1:
                hop(cross(k + 1, way), s, src, toward[way]).start()
            elif s == way:
                hop(cross(half), s, src, toward[way]).start()

    def arrive_both(b):
        for s in range(2):
            arrive(b, s)

    both = [True, True]
    neither = [False, False]

    arrive_own(1)
    arrive_both(cross(0))
    if half > 2:
        arrive_own(2)
    for o in range(1, tp_count):
        map_spread(t, (t + o) % tp_count).wait_recv()
    project(0, [z, z], [True, False])
    if half > 2:
        project(own(1), ahead(1), both)
    for k in range(3, half):
        arrive_own(k)
        arrive_cross(k - 2)
        if k == 3:
            finish_own(z, True)
            finish_cross(z)
        project(own(k - 1), ahead(k - 1), both)
        project(cross(k - 2), ahead(k - 2), neither)
        for zz in ahead(k - 2):
            finish_own(zz)
    for i in range(prompts):
        uv_out[i] = uv[adapters[t * prompts + i]]
    uv_copy = remote(uv_out, uv_in, uv_sems.at[0], uv_sems.at[1], req=pair)
    uv_copy.start()
    arrive_both(own(half))
    project(own(half - 1), ahead(half - 1) + [far], [True] * 3)
    if half > 2:
        arrive_cross(half - 2)
        for zz in ahead(half - 2):
            finish_own(zz)
        for zz in ahead(half - 1) + [far]:
            finish_own(zz)
        project(cross(half - 2), ahead(half - 2), neither)
        if half > 3:
            for zz in ahead(half - 3):
                finish_cross(zz)
        else:
            finish_own(z, True)
            finish_cross(z)
    else:
        finish_own(z, True)
        finish_cross(z)
        for zz in ahead(half - 1) + [far]:
            finish_own(zz)
    arrive_cross(half - 1)

    def others(body):
        def one(o, _):
            body((r + o) % req_count)
            return 0

        lax.fori_loop(1, req_count, one, 0)

    def column(body):
        def one(o, _):
            body((z + o) % ring)
            return 0

        lax.fori_loop(1, ring, one, 0)

    def rank_copy(target, slot):
        return remote(
            rank_all.at[slot], rank_all.at[slot], rank_send.at[target], rank_recv.at[slot], req=target
        )

    column(lambda zz: low_arrival(zz).wait_recv())
    low = low_in[0].astype(F32)
    for zz in range(1, ring):
        low = low + low_in[zz].astype(F32)
    rank_all[r] = low.astype(BF16)
    others(lambda target: rank_copy(target, r).start())

    project(cross(half - 1), ahead(half - 1), neither)
    if half > 2:
        for zz in ahead(half - 2):
            finish_cross(zz)
    arrive_both(cross(half))
    project(cross(half), [far], [False], late=True)

    def step_copy(i):
        target = t * per_dev + i
        return remote(
            msg_ref.at[i],
            step_in.at[r % per_dev],
            step_send.at[i],
            step_got.at[r % per_dev],
            req=target,
            tp=r // per_dev,
        )

    def step_self(i):
        return (t * per_dev + i == r) & (r // per_dev == t)

    for i in range(per_dev):

        @pl.when(step_self(i))
        def _():
            step_in[r % per_dev] = msg_ref[i]

        @pl.when(jnp.logical_not(step_self(i)))
        def _():
            step_copy(i).start()

    for zz in ahead(half - 1):
        finish_cross(zz)
    b_copy(far).wait_recv()
    kv_own[1 - h, far] = b_own[far] + b_in[far].astype(F32)
    for i in range(2):
        late_copy(i).wait_recv()
    uv_copy.wait_recv()
    for hh in range(2):
        for zz in range(ring):
            there = (hh == 1 - h) & (zz == pair_far)

            @pl.when(jnp.logical_not(there))
            def _():
                kv_copy(hh, zz).wait_recv()
                kv_oth[hh, zz] = kv_in[hh, zz].astype(F32)

            @pl.when(there)
            def _():
                kv_oth[hh, zz] = late_in[0].astype(F32) + late_in[1].astype(F32)

    others(lambda source: rank_copy(source, source).wait_recv())
    for source in range(req_count):
        packed = rank_all[source].astype(F32)
        ranks[source, :part] = packed
        ranks[source, part:] = pltpu.roll(packed, HEAD // 2, 1)

    even = r % 2 == 0
    slots = req_count * SLOTS
    share = slots // 2
    low_lane = lax.broadcasted_iota(jnp.int32, (slots, HEAD), 1) < HEAD // 2
    scale = HEAD ** (-0.5)

    def assemble(n):
        at = pl.ds(pl.multiple_of(n * SLOTS, SLOTS), SLOTS)
        mine = kv_own[:, :, at, :].reshape(slots, HEAD)
        theirs = kv_oth[:, :, at, :].reshape(slots, HEAD)
        first = jnp.where(even, mine, theirs)
        second = jnp.where(even, theirs, mine)
        k = jnp.where(low_lane, first, pltpu.roll(second, HEAD // 2, 1)).astype(BF16)
        v = jnp.where(low_lane, pltpu.roll(first, HEAD // 2, 1), second)
        uv_mine, uv_theirs = uv_out[n], uv_in[n]
        up_v = jnp.concatenate(
            [jnp.where(even, uv_mine, uv_theirs), jnp.where(even, uv_theirs, uv_mine)], axis=1
        )
        rank_rows = ranks[:, at, :].reshape(slots, HEAD).astype(BF16)
        v = v + jnp.dot(rank_rows[:, rank:maps], up_v, preferred_element_type=F32)
        k_full[n] = k
        v_full[n] = v.astype(BF16)

    steps = step_out.shape[1] // heads
    qrows = heads * steps

    def step_arrival(j):
        source_req = t * per_dev + j
        return remote(
            msg_ref.at[0],
            step_in.at[j],
            step_send.at[0],
            step_got.at[j],
            req=source_req,
            tp=r // per_dev,
        )

    def out_copy(j, target):
        return remote(
            step_out.at[j],
            step_recv.at[r],
            out_send.at[j, target],
            out_got.at[r],
            req=t * per_dev + j,
            tp=target,
        )

    def out_arrival(source):
        return remote(
            step_out.at[0],
            step_recv.at[source],
            out_send.at[0, 0],
            out_got.at[source],
            req=source,
            tp=r // per_dev,
        )

    for j in range(per_dev):

        @pl.when(jnp.logical_not((t * per_dev + j == r) & (r // per_dev == t)))
        def _():
            step_arrival(j).wait_recv()

        n = 2 * j + p
        assemble(n)
        length = lens[t * prompts + n]
        k, v = k_full[n], v_full[n]
        got = step_in[j]
        qs = got[:qrows]
        tail = got[qrows:].astype(F32)
        new_k = tail[:SLOTS].astype(BF16)
        new_v = tail[SLOTS : 2 * SLOTS].astype(BF16)
        s_old = lax.dot_general(qs, k, (((1,), (1,)), ((), ())), preferred_element_type=F32) * scale
        s_new = (
            lax.dot_general(qs, new_k, (((1,), (1,)), ((), ())), preferred_element_type=F32) * scale
        )
        s_old = jnp.where(lax.broadcasted_iota(jnp.int32, (qrows, slots), 1) < length, s_old, NEG)
        at_step = lax.broadcasted_iota(jnp.int32, (qrows, SLOTS), 0) % steps
        at_new = lax.broadcasted_iota(jnp.int32, (qrows, SLOTS), 1)
        s_new = jnp.where(at_new <= at_step, s_new, NEG)
        top = jnp.maximum(
            jnp.max(s_old, axis=1, keepdims=True), jnp.max(s_new, axis=1, keepdims=True)
        )
        e_old, e_new = jnp.exp(s_old - top), jnp.exp(s_new - top)
        total = jnp.sum(e_old, axis=1, keepdims=True) + jnp.sum(e_new, axis=1, keepdims=True)
        mixed = jnp.zeros((qrows, HEAD), F32)
        for e, values in ((e_old, v), (e_new, new_v)):
            coarse = e.astype(BF16)
            fine = (e - coarse.astype(F32)).astype(BF16)
            mixed = mixed + jnp.dot(coarse, values, preferred_element_type=F32)
            mixed = mixed + jnp.dot(fine, values, preferred_element_type=F32)
        step_out[j] = (mixed / total).astype(BF16)
        for o in range(tp_count):
            target = (t + o) % tp_count
            if o == 0:

                @pl.when(t * per_dev + j == r)
                def _():
                    step_recv[r] = step_out[j]

                @pl.when(t * per_dev + j != r)
                def _():
                    out_copy(j, t).start()
            else:
                out_copy(j, target).start()

    for j in range(per_dev):
        assemble(2 * j + 1 - p)
    for zz in range(ring):
        q_copy(zz).wait_recv()
    base_q = (q_keep[...] + q_in[...].astype(F32)).reshape(ring, prompts, SLOTS, cols)
    my_ranks = ranks[pl.ds(p * ring, ring)].reshape(ring, prompts, SLOTS, HEAD)
    row_pos = lax.broadcasted_iota(jnp.int32, (heads * share, slots), 0) % share + p * share
    col_pos = lax.broadcasted_iota(jnp.int32, (heads * share, slots), 1)
    out_pos = lax.broadcasted_iota(jnp.int32, (heads * share, HEAD), 0) % share + p * share
    for i in range(prompts):
        length = lens[t * prompts + i]
        adapter = adapters[t * prompts + i]
        k, v = k_full[i], v_full[i]
        rank_q = my_ranks[:, i].reshape(share, HEAD).astype(BF16)[:, :rank]
        q = base_q[:, i].reshape(share, cols) + jnp.dot(
            rank_q, uq[adapter], preferred_element_type=F32
        )
        q = q.astype(BF16)
        q = jnp.concatenate([q[:, g * HEAD : (g + 1) * HEAD] for g in range(heads)], axis=0)
        s = lax.dot_general(q, k, (((1,), (1,)), ((), ())), preferred_element_type=F32) * scale
        s = jnp.where((col_pos <= row_pos) & (col_pos < length), s, NEG)
        e = jnp.exp(s - jnp.max(s, axis=1, keepdims=True))
        w = (e / jnp.sum(e, axis=1, keepdims=True)).astype(BF16)
        o = jnp.dot(w, v, preferred_element_type=F32)
        o = jnp.where(out_pos < length, o, 0.0).astype(BF16)
        for g in range(heads):
            prefill_ref[i, :, g * HEAD : (g + 1) * HEAD] = o[g * share : (g + 1) * share]

    for b in range(1, 2 * ring):
        for s in range(2):
            hop(b, s, own_piece(s), above).wait_send()
    for target in range(tp_count):
        map_spread(target, t).wait_send()
    for zz in range(ring):
        q_copy(zz).wait_send()
        a_copy(zz).wait_send()
        b_copy(zz).wait_send()
        for hh in range(2):

            @pl.when(jnp.logical_not((hh == 1 - h) & (zz == far)))
            def _():
                kv_copy(hh, zz).wait_send()

    for i in range(2):
        late_copy(i).wait_send()
    column(lambda zz: low_copy(zz).wait_send())
    others(lambda target: rank_copy(target, r).wait_send())
    uv_copy.wait_send()
    for i in range(per_dev):

        @pl.when(jnp.logical_not(step_self(i)))
        def _():
            step_copy(i).wait_send()

    for j in range(per_dev):
        for target in range(tp_count):

            @pl.when(jnp.logical_not((t * per_dev + j == r) & (target == t)))
            def _():
                out_copy(j, target).wait_send()

    def got_out(source, _):
        @pl.when(jnp.logical_not((source == r) & (r // per_dev == t)))
        def _():
            out_arrival(source).wait_recv()

        return 0

    lax.fori_loop(0, req_count, got_out, 0)
    decoded_ref[...] = step_recv[...]


def local(
    prompt_states,
    prompt_lengths,
    adapter_ids,
    w_query,
    w_key,
    value_weight,
    down_query,
    up_query,
    down_value,
    value_up_weight,
    step_queries,
    step_keyvals,
):
    req_count, tp_count = lax.axis_size("req"), lax.axis_size("tp")
    t = lax.axis_index("tp")
    prompts, slots, width = prompt_states.shape
    rows = prompts * slots
    cols = w_query.shape[1]
    kv_cols = w_key.shape[1]
    rank = down_query.shape[2]
    adapter_count = up_query.shape[0]
    ring = req_count // 2
    heads = cols // HEAD
    steps = step_queries.shape[1]
    per_dev = req_count // tp_count
    total_slots = req_count * slots

    qs = lax.dynamic_slice_in_dim(step_queries[0], t * per_dev * cols, per_dev * cols, 1)
    qs = qs.reshape(steps, per_dev, heads, HEAD).transpose(1, 2, 0, 3)
    qs = qs.reshape(per_dev, heads * steps, HEAD)
    kv = lax.dynamic_slice_in_dim(
        step_keyvals[0], t * per_dev * kv_cols, per_dev * kv_cols, 2
    ).reshape(steps, 2, per_dev // 2, HEAD)
    kv = jnp.repeat(kv.transpose(2, 1, 0, 3), 2, axis=0)
    kv = jnp.pad(kv, ((0, 0), (0, 0), (0, SLOTS - steps), (0, 0))).reshape(per_dev, 2 * SLOTS, HEAD)
    message = jnp.concatenate([qs, kv], axis=1)

    vmem = pl.BlockSpec(memory_space=pltpu.VMEM)
    smem = pl.BlockSpec(memory_space=pltpu.SMEM)
    hbm = pl.BlockSpec(memory_space=pl.ANY)
    dma = pltpu.SemaphoreType.DMA
    prefill, decoded = pl.pallas_call(
        functools.partial(kernel, req_count, tp_count),
        out_shape=(
            jax.ShapeDtypeStruct((prompts, total_slots // 2, cols), BF16),
            jax.ShapeDtypeStruct((req_count, heads * steps, HEAD), BF16),
        ),
        in_specs=[smem, smem] + [hbm] * 8 + [vmem],
        out_specs=(vmem, vmem),
        scratch_shapes=[
            pltpu.VMEM((req_count * rows, width), BF16),
            pltpu.VMEM((width, cols), BF16),
            pltpu.VMEM((SIDE, width), BF16),
            pltpu.VMEM((adapter_count, rank, cols), BF16),
            pltpu.VMEM((adapter_count, rank, kv_cols), BF16),
            pltpu.VMEM((ring, rows, cols), F32),
            pltpu.VMEM((ring, rows, cols), BF16),
            pltpu.VMEM((ring, rows, cols), BF16),
            pltpu.VMEM((ring, rows, SIDE), F32),
            pltpu.VMEM((ring, rows, SIDE), BF16),
            pltpu.VMEM((ring, rows, SIDE), BF16),
            pltpu.VMEM((ring, rows, HEAD), F32),
            pltpu.VMEM((ring, rows, HEAD), BF16),
            pltpu.VMEM((ring, rows, HEAD), BF16),
            pltpu.VMEM((2, ring, rows, HEAD), F32),
            pltpu.VMEM((2, ring, rows, HEAD), F32),
            pltpu.VMEM((2, ring, rows, HEAD), BF16),
            pltpu.VMEM((2, ring, rows, HEAD), BF16),
            pltpu.VMEM((2, rows, HEAD), BF16),
            pltpu.VMEM((ring, rows // 2, HEAD), BF16),
            pltpu.VMEM((ring, rows // 2, HEAD), BF16),
            pltpu.VMEM((req_count, rows // 2, HEAD), BF16),
            pltpu.VMEM((req_count, rows, HEAD), F32),
            pltpu.VMEM((prompts, rank, kv_cols), BF16),
            pltpu.VMEM((prompts, rank, kv_cols), BF16),
            pltpu.VMEM((prompts, total_slots, HEAD), BF16),
            pltpu.VMEM((prompts, total_slots, HEAD), BF16),
            pltpu.VMEM((per_dev, heads * steps + 2 * SLOTS, HEAD), BF16),
            pltpu.VMEM((per_dev, heads * steps, HEAD), BF16),
            pltpu.VMEM((req_count, heads * steps, HEAD), BF16),
            dma((8,)),
            dma((req_count, 2)),
            dma((req_count, 2)),
            dma((tp_count,)),
            dma((tp_count,)),
            dma((ring,)),
            dma((ring,)),
            dma((ring,)),
            dma((ring,)),
            dma((ring,)),
            dma((ring,)),
            dma((2, ring)),
            dma((2, ring)),
            dma((2,)),
            dma((2,)),
            dma((ring,)),
            dma((ring,)),
            dma((req_count,)),
            dma((req_count,)),
            dma((2,)),
            dma((per_dev,)),
            dma((per_dev,)),
            dma((per_dev, tp_count)),
            dma((req_count,)),
        ],
        compiler_params=pltpu.CompilerParams(
            collective_id=0, has_side_effects=True, vmem_limit_bytes=56 * 1024 * 1024
        ),
        cost_estimate=pl.CostEstimate(
            flops=2 * req_count * rows * width * (cols + SIDE),
            bytes_accessed=2 * width * (cols + SIDE),
            transcendentals=0,
        ),
    )(
        prompt_lengths,
        adapter_ids,
        prompt_states.reshape(rows, width),
        w_query,
        w_key.T,
        value_weight.T,
        down_query[0].T,
        down_value[0].T,
        up_query,
        value_up_weight,
        message,
    )
    decoded = decoded.reshape(req_count, heads, steps, HEAD).transpose(2, 0, 1, 3)
    return prefill, decoded.reshape(1, steps, req_count * cols)


def solution(mesh):
    in_specs = (
        P("tp", "req", "pp"),
        P(),
        P(),
        P("pp", "req"),
        P("pp", "req"),
        P("pp", "req"),
        P("req", "pp", None),
        P(None, None, "req"),
        P("req", "pp", None),
        P(None, None, "req"),
        P(("req", "pp"), None, None),
        P(("req", "pp"), None, None, None),
    )
    out_specs = (P("tp", "pp", "req"), P(("req", "pp"), None, None))
    return jax.shard_map(local, mesh=mesh, in_specs=in_specs, out_specs=out_specs, check_vma=False)
```

time: 91.4 us -> 73.5 us (0.80)
  Pallas kernels: 85.9 us -> 68 us
    pallas_call x1, Pallas kernels: 85.9 us -> 68 us  [local(): pl.pallas_call(functools.partial(kernel, req_count, tp_count), out_shape=...]
where the time goes in v3:
time: 73.5 us; the launch traced here: 73.3 us
  Pallas kernels  68 us (93%)
  local copies, waits for them, and re-layouts  4 us (5%)
    pallas_call x1, Pallas kernels, local(): pl.pallas_call(functools.partial(kernel, req_count, tp_count), out_shape=...  68 us
    unnamed x4, local copies, waits for them, and re-layouts  3.25 us

profile of v3, /device:TPU:1, one launch (start us, length us, event | category | flops | bytes accessed | tf_op | source)
XLA Modules:
  0.0 73.3 jit_solution(10858020111384220099)
XLA Ops:
  0.6 0.0 copy-start
  0.7 0.7 dynamic-slice_bitcast_fusion
  1.4 0.1 copy-done
  1.5 0.6 pad_maximum_fusion.msg_ref
  2.1 68.0 %shard_map.131 = (bf16[4,64,512]{2,1,0:T(8,128)(2,1)}, bf16[16,16,128]{2,1,0:T(8,128)(2,1)}) custom-call(s32[32]{0:T(128)} %lens.1, s32[32]{0:T(128)} %adapters.1, bf16[32,4096]{1,0:T(8,128)(2,1)} %bitcast.33, bf16[4096,512]{1,0:T(8,128)(2,1)} %wq_hbm.1, bf16[64,4096]{1,0:T(8,128)(2,1)} %bitcast.31, bf16[64,4096]{1,0:T(8,128)(2,1)} %bitcast.32, ...), custom_call_target="tpu_custom_call" | custom-call | flops 3221225472 | bytes 6291456 | tf_op jit(solution)/shard_map/pallas_call | solution.py:705
  70.1 1.7 %copy.22 = bf16[4,64,512]{2,1,0:T(8,128)(2,1)} copy(bf16[4,64,512]{2,1,0:T(8,128)(2,1)} %get-tuple-element.8) | data formatting | bytes 524288
  71.8 1.5 %copy.23 = bf16[1,4,8192]{2,1,0:T(4,128)(2,1)} copy(bf16[1,4,8192]{2,1,0:T(4,128)(2,1)} %bitcast.28) | data formatting | bytes 131072
  (4 shorter events, 0.0 us)
Async XLA Ops:
  0.6 0.8 %copy-start = (bf16[1,4,8192]{2,1,0:T(4,128)(2,1)S(1)}, bf16[1,4,8192]{2,1,0:T(4,128)(2,1)}, u32[]{:S(2)}) copy-start(bf16[1,4,8192]{2,1,0:T(4,128)(2,1)} %param.22) | copy-start | bytes 196612

commit v4 on v3

--- a/solution.py
+++ b/solution.py
@@ -29,9 +29,14 @@
     dv_hbm,
     uq_hbm,
     uv_hbm,
-    msg_ref,
+    sq_hbm,
+    skv_hbm,
     prefill_ref,
     decoded_ref,
+    msg_ref,
+    msg_f32,
+    sq,
+    skv,
     blocks,
     weights,
     side_w,
@@ -96,7 +101,7 @@
     prompts = rows // SLOTS
     cols = q_keep.shape[2]
     heads = cols // HEAD
-    per_dev = msg_ref.shape[0]
+    per_dev = req_count // tp_count
     kv_cols, rank = wk_hbm.shape[0], dq_hbm.shape[0]
     maps = 2 * rank
     above = h * ring + (z + 1) % ring
@@ -105,7 +110,7 @@
     other = 1 - p
     pair = r + 1 - 2 * (r % 2)
     far = (z + half) % ring
-    pair_far = (pair % ring + half) % ring
+    pair_late = [(pair + ring - half + 1) % ring, (pair + half - 1) % ring]
 
     def remote(src, dst, send, recv, req=None, tp=None, pp=None):
         where = (r if req is None else req, t if tp is None else tp, p if pp is None else pp)
@@ -130,6 +135,8 @@
                 (wq_hbm, weights),
                 (uq_hbm, uq),
                 (uv_hbm, uv),
+                (sq_hbm, sq),
+                (skv_hbm, skv),
             ]
         )
     ]
@@ -216,12 +223,12 @@
     def b_copy(zz):
         return remote(b_out.at[zz], b_in.at[zz], b_send.at[zz], b_recv.at[zz], pp=other)
 
-    def late_copy(i):
-        return remote(
-            b_out.at[far],
-            late_in.at[i],
-            late_send.at[i],
-            late_recv.at[i],
+    def late_copy(i, d):
+        return remote(
+            b_out.at[ahead(half - 1)[d]],
+            late_in.at[i, d],
+            late_send.at[i, d],
+            late_recv.at[i, d],
             req=pair,
             pp=(p, other)[i],
         )
@@ -247,8 +254,8 @@
                 b_out[zz] = block[:, :HEAD].astype(BF16)
                 b_copy(zz).start()
                 if late:
-                    late_copy(0).start()
-                    late_copy(1).start()
+                    late_copy(0, i).start()
+                    late_copy(1, i).start()
 
         def part_of(n, _):
             lanes = pl.ds(pl.multiple_of(n * SIDE, SIDE), SIDE)
@@ -336,7 +343,7 @@
             elif s == way:
                 hop(own(half), s, src, toward[way]).start()
             if k == 1:
-                hop(cross(1, way), s, src, across).start()
+                hop(cross(k, way), s, src, across).start()
 
     def arrive_cross(k):
         for way, s in order:
@@ -344,12 +351,26 @@
             src = piece(cross(k, way), s)
             if k < half - 1:
                 hop(cross(k + 1, way), s, src, toward[way]).start()
-            elif s == way:
-                hop(cross(half), s, src, toward[way]).start()
 
     def arrive_both(b):
         for s in range(2):
             arrive(b, s)
+
+    def make_messages():
+        steps = sq.shape[1]
+        msg_f32[...] = jnp.zeros(msg_f32.shape, F32)
+        for i in range(per_dev):
+            head = t * per_dev + i
+            for g in range(heads):
+                lanes = pl.ds(pl.multiple_of(head * cols + g * HEAD, HEAD), HEAD)
+                msg_f32[i, g * steps : (g + 1) * steps] = sq[0, :, lanes].astype(F32)
+            lanes = pl.ds(pl.multiple_of((head // 2) * HEAD, HEAD), HEAD)
+            for s in range(steps):
+                new = skv[0, s, :, lanes].astype(F32)
+                first = heads * steps + s
+                msg_f32[i, first : first + 1] = new[0:1]
+                msg_f32[i, first + SLOTS : first + SLOTS + 1] = new[1:2]
+        msg_ref[...] = msg_f32[...].astype(BF16)
 
     both = [True, True]
     neither = [False, False]
@@ -363,6 +384,7 @@
     project(0, [z, z], [True, False])
     if half > 2:
         project(own(1), ahead(1), both)
+    make_messages()
     for k in range(3, half):
         arrive_own(k)
         arrive_cross(k - 2)
@@ -377,7 +399,9 @@
         uv_out[i] = uv[adapters[t * prompts + i]]
     uv_copy = remote(uv_out, uv_in, uv_sems.at[0], uv_sems.at[1], req=pair)
     uv_copy.start()
-    arrive_both(own(half))
+    for s in range(2):
+        arrive(own(half), s)
+        hop(cross(half), s, piece(own(half), s), across).start()
     project(own(half - 1), ahead(half - 1) + [far], [True] * 3)
     if half > 2:
         arrive_cross(half - 2)
@@ -397,21 +421,20 @@
         finish_cross(z)
         for zz in ahead(half - 1) + [far]:
             finish_own(zz)
-    arrive_cross(half - 1)
+    arrive_both(cross(half))
+    project(cross(half), [far], [False])
+
+    distances = sorted(range(ring), key=lambda o: -min(o, ring - o))
 
     def others(body):
-        def one(o, _):
-            body((r + o) % req_count)
-            return 0
-
-        lax.fori_loop(1, req_count, one, 0)
+        for o in distances:
+            body((1 - h) * ring + (z + o) % ring)
+            if o > 0:
+                body(h * ring + (z + o) % ring)
 
     def column(body):
-        def one(o, _):
+        for o in distances[:-1]:
             body((z + o) % ring)
-            return 0
-
-        lax.fori_loop(1, ring, one, 0)
 
     def rank_copy(target, slot):
         return remote(
@@ -425,12 +448,11 @@
     rank_all[r] = low.astype(BF16)
     others(lambda target: rank_copy(target, r).start())
 
-    project(cross(half - 1), ahead(half - 1), neither)
     if half > 2:
         for zz in ahead(half - 2):
             finish_cross(zz)
-    arrive_both(cross(half))
-    project(cross(half), [far], [False], late=True)
+    arrive_cross(half - 1)
+    project(cross(half - 1), ahead(half - 1), neither, late=True)
 
     def step_copy(i):
         target = t * per_dev + i
@@ -456,25 +478,25 @@
         def _():
             step_copy(i).start()
 
+    finish_cross(far)
     for zz in ahead(half - 1):
-        finish_cross(zz)
-    b_copy(far).wait_recv()
-    kv_own[1 - h, far] = b_own[far] + b_in[far].astype(F32)
+        b_copy(zz).wait_recv()
+        kv_own[1 - h, zz] = b_own[zz] + b_in[zz].astype(F32)
     for i in range(2):
-        late_copy(i).wait_recv()
+        for d in range(2):
+            late_copy(i, d).wait_recv()
     uv_copy.wait_recv()
     for hh in range(2):
         for zz in range(ring):
-            there = (hh == 1 - h) & (zz == pair_far)
-
-            @pl.when(jnp.logical_not(there))
+            there = [(hh == 1 - h) & (zz == late_zz) for late_zz in pair_late]
+
+            @pl.when(jnp.logical_not(there[0] | there[1]))
             def _():
                 kv_copy(hh, zz).wait_recv()
                 kv_oth[hh, zz] = kv_in[hh, zz].astype(F32)
 
-            @pl.when(there)
-            def _():
-                kv_oth[hh, zz] = late_in[0].astype(F32) + late_in[1].astype(F32)
+    for d in range(2):
+        kv_oth[1 - h, pair_late[d]] = late_in[0, d].astype(F32) + late_in[1, d].astype(F32)
 
     others(lambda source: rank_copy(source, source).wait_recv())
     for source in range(req_count):
@@ -574,7 +596,7 @@
             mixed = mixed + jnp.dot(coarse, values, preferred_element_type=F32)
             mixed = mixed + jnp.dot(fine, values, preferred_element_type=F32)
         step_out[j] = (mixed / total).astype(BF16)
-        for o in range(tp_count):
+        for o in sorted(range(tp_count), key=lambda o: -min(o, tp_count - o)):
             target = (t + o) % tp_count
             if o == 0:
 
@@ -627,12 +649,15 @@
         b_copy(zz).wait_send()
         for hh in range(2):
 
-            @pl.when(jnp.logical_not((hh == 1 - h) & (zz == far)))
+            mine = [(hh == 1 - h) & (zz == late_zz) for late_zz in ahead(half - 1)]
+
+            @pl.when(jnp.logical_not(mine[0] | mine[1]))
             def _():
                 kv_copy(hh, zz).wait_send()
 
     for i in range(2):
-        late_copy(i).wait_send()
+        for d in range(2):
+            late_copy(i, d).wait_send()
     column(lambda zz: low_copy(zz).wait_send())
     others(lambda target: rank_copy(target, r).wait_send())
     uv_copy.wait_send()
@@ -658,6 +683,17 @@
 
     lax.fori_loop(0, req_count, got_out, 0)
     decoded_ref[...] = step_recv[...]
+
+
+def deliver(prefill_in, decoded_in, prefill_ref, decoded_ref):
+    prefill_ref[...] = prefill_in[...]
+    steps = decoded_ref.shape[1]
+    heads = decoded_in.shape[1] // steps
+    for source in range(decoded_in.shape[0]):
+        got = decoded_in[source].astype(F32)
+        for g in range(heads):
+            lanes = pl.ds((source * heads + g) * HEAD, HEAD)
+            decoded_ref[0, :, lanes] = got[g * steps : (g + 1) * steps].astype(BF16)
 
 
 def local(
@@ -675,7 +711,6 @@
     step_keyvals,
 ):
     req_count, tp_count = lax.axis_size("req"), lax.axis_size("tp")
-    t = lax.axis_index("tp")
     prompts, slots, width = prompt_states.shape
     rows = prompts * slots
     cols = w_query.shape[1]
@@ -688,16 +723,6 @@
     per_dev = req_count // tp_count
     total_slots = req_count * slots
 
-    qs = lax.dynamic_slice_in_dim(step_queries[0], t * per_dev * cols, per_dev * cols, 1)
-    qs = qs.reshape(steps, per_dev, heads, HEAD).transpose(1, 2, 0, 3)
-    qs = qs.reshape(per_dev, heads * steps, HEAD)
-    kv = lax.dynamic_slice_in_dim(
-        step_keyvals[0], t * per_dev * kv_cols, per_dev * kv_cols, 2
-    ).reshape(steps, 2, per_dev // 2, HEAD)
-    kv = jnp.repeat(kv.transpose(2, 1, 0, 3), 2, axis=0)
-    kv = jnp.pad(kv, ((0, 0), (0, 0), (0, SLOTS - steps), (0, 0))).reshape(per_dev, 2 * SLOTS, HEAD)
-    message = jnp.concatenate([qs, kv], axis=1)
-
     vmem = pl.BlockSpec(memory_space=pltpu.VMEM)
     smem = pl.BlockSpec(memory_space=pltpu.SMEM)
     hbm = pl.BlockSpec(memory_space=pl.ANY)
@@ -708,9 +733,13 @@
             jax.ShapeDtypeStruct((prompts, total_slots // 2, cols), BF16),
             jax.ShapeDtypeStruct((req_count, heads * steps, HEAD), BF16),
         ),
-        in_specs=[smem, smem] + [hbm] * 8 + [vmem],
+        in_specs=[smem, smem] + [hbm] * 10,
         out_specs=(vmem, vmem),
         scratch_shapes=[
+            pltpu.VMEM((per_dev, heads * steps + 2 * SLOTS, HEAD), BF16),
+            pltpu.VMEM((per_dev, heads * steps + 2 * SLOTS, HEAD), F32),
+            pltpu.VMEM(step_queries.shape, BF16),
+            pltpu.VMEM(step_keyvals.shape, BF16),
             pltpu.VMEM((req_count * rows, width), BF16),
             pltpu.VMEM((width, cols), BF16),
             pltpu.VMEM((SIDE, width), BF16),
@@ -729,7 +758,7 @@
             pltpu.VMEM((2, ring, rows, HEAD), F32),
             pltpu.VMEM((2, ring, rows, HEAD), BF16),
             pltpu.VMEM((2, ring, rows, HEAD), BF16),
-            pltpu.VMEM((2, rows, HEAD), BF16),
+            pltpu.VMEM((2, 2, rows, HEAD), BF16),
             pltpu.VMEM((ring, rows // 2, HEAD), BF16),
             pltpu.VMEM((ring, rows // 2, HEAD), BF16),
             pltpu.VMEM((req_count, rows // 2, HEAD), BF16),
@@ -741,7 +770,7 @@
             pltpu.VMEM((per_dev, heads * steps + 2 * SLOTS, HEAD), BF16),
             pltpu.VMEM((per_dev, heads * steps, HEAD), BF16),
             pltpu.VMEM((req_count, heads * steps, HEAD), BF16),
-            dma((8,)),
+            dma((10,)),
             dma((req_count, 2)),
             dma((req_count, 2)),
             dma((tp_count,)),
@@ -754,8 +783,8 @@
             dma((ring,)),
             dma((2, ring)),
             dma((2, ring)),
-            dma((2,)),
-            dma((2,)),
+            dma((2, 2)),
+            dma((2, 2)),
             dma((ring,)),
             dma((ring,)),
             dma((req_count,)),
@@ -785,10 +814,18 @@
         down_value[0].T,
         up_query,
         value_up_weight,
-        message,
+        step_queries,
+        step_keyvals,
     )
-    decoded = decoded.reshape(req_count, heads, steps, HEAD).transpose(2, 0, 1, 3)
-    return prefill, decoded.reshape(1, steps, req_count * cols)
+    return pl.pallas_call(
+        deliver,
+        out_shape=(
+            jax.ShapeDtypeStruct(prefill.shape, BF16),
+            jax.ShapeDtypeStruct(step_queries.shape, BF16),
+        ),
+        in_specs=[vmem, vmem],
+        out_specs=(vmem, vmem),
+    )(prefill, decoded)
 
 
 def solution(mesh):

time: 73.5 us -> 69.2 us (0.941)
  local copies, waits for them, and re-layouts: 4 us -> 0 us
    unnamed x4 -> x0, local copies, waits for them, and re-layouts: 3.25 us -> none
    pallas_call x0 -> x1, Pallas kernels: none -> 1.7 us  [local(): pl.pallas_call(deliver, out_shape=(jax.ShapeDtypeStruct(prefill.shape, BF...]
    pallas_call x1, Pallas kernels: 68 us -> 66.7 us  [local(): pl.pallas_call(functools.partial(kernel, req_count, tp_count), out_shape=...]
where the time goes in v4:
time: 69.2 us; the launch traced here: 69 us
  Pallas kernels  68.4 us (99%)
    pallas_call x1, Pallas kernels, local(): pl.pallas_call(functools.partial(kernel, req_count, tp_count), out_shape=...  66.7 us
    pallas_call x1, Pallas kernels, local(): pl.pallas_call(deliver, out_shape=(jax.ShapeDtypeStruct(prefill.shape, BF...  1.7 us

profile of v4, /device:TPU:1, one launch (start us, length us, event | category | flops | bytes accessed | tf_op | source)
XLA Modules:
  0.0 69.0 jit_solution(6059232435471606826)
XLA Ops:
  0.6 66.7 %shard_map.131 = (bf16[4,64,512]{2,1,0:T(8,128)(2,1)}, bf16[16,16,128]{2,1,0:T(8,128)(2,1)}) custom-call(s32[32]{0:T(128)} %lens.1, s32[32]{0:T(128)} %adapters.1, bf16[32,4096]{1,0:T(8,128)(2,1)} %bitcast.11, bf16[4096,512]{1,0:T(8,128)(2,1)} %wq_hbm.1, bf16[64,4096]{1,0:T(8,128)(2,1)} %bitcast.9, bf16[64,4096]{1,0:T(8,128)(2,1)} %bitcast.10, ...), custom_call_target="tpu_custom_call" | custom-call | flops 3221225472 | bytes 6291456 | tf_op jit(solution)/shard_map/pallas_call | solution.py:730
  67.3 1.7 %shard_map.132 = (bf16[4,64,512]{2,1,0:T(8,128)(2,1)}, bf16[1,4,8192]{2,1,0:T(4,128)(2,1)}) custom-call(bf16[4,64,512]{2,1,0:T(8,128)(2,1)} %get-tuple-element.4.prefill_in, bf16[16,16,128]{2,1,0:T(8,128)(2,1)} %get-tuple-element.5.decoded_in), custom_call_target="tpu_custom_call" | custom-call | tf_op jit(solution)/shard_map/pallas_call | solution.py:820

commit v5 on v4

--- a/solution.py
+++ b/solution.py
@@ -91,6 +91,7 @@
     step_got,
     out_send,
     out_got,
+    hello,
 ):
     r, t, p = lax.axis_index("req"), lax.axis_index("tp"), lax.axis_index("pp")
     ring = req_count // 2
@@ -210,152 +211,6 @@
         hop(cross(0), s, own_piece(s), across).start()
     for load in loads[2:]:
         load.wait()
-    map_hop().wait_recv()
-    for o in range(1, tp_count):
-        map_spread((t + o) % tp_count, t).start()
-
-    def q_copy(zz):
-        return remote(q_out.at[zz], q_in.at[zz], q_send.at[zz], q_recv.at[zz], pp=other)
-
-    def a_copy(zz):
-        return remote(a_out.at[zz], a_in.at[zz], a_send.at[zz], a_recv.at[zz], pp=other)
-
-    def b_copy(zz):
-        return remote(b_out.at[zz], b_in.at[zz], b_send.at[zz], b_recv.at[zz], pp=other)
-
-    def late_copy(i, d):
-        return remote(
-            b_out.at[ahead(half - 1)[d]],
-            late_in.at[i, d],
-            late_send.at[i, d],
-            late_recv.at[i, d],
-            req=pair,
-            pp=(p, other)[i],
-        )
-
-    def project(first, places, in_own, late=False):
-        count = len(places) * rows
-        at = pl.ds(first * rows, count)
-        side = SIDE if any(in_own) else HEAD
-        got = lax.dot_general(
-            blocks[at, :],
-            side_w[:side],
-            (((1,), (1,)), ((), ())),
-            preferred_element_type=F32,
-        )
-        for i, (zz, mine) in enumerate(zip(places, in_own)):
-            block = got[i * rows : (i + 1) * rows]
-            if mine:
-                a_own[zz] = block
-                a_out[zz] = block.astype(BF16)
-                a_copy(zz).start()
-            else:
-                b_own[zz] = block[:, :HEAD]
-                b_out[zz] = block[:, :HEAD].astype(BF16)
-                b_copy(zz).start()
-                if late:
-                    late_copy(0, i).start()
-                    late_copy(1, i).start()
-
-        def part_of(n, _):
-            lanes = pl.ds(pl.multiple_of(n * SIDE, SIDE), SIDE)
-            got = jnp.dot(blocks[at, :], weights[:, lanes], preferred_element_type=F32)
-            for i, (zz, mine) in enumerate(zip(places, in_own)):
-                block = got[i * rows : (i + 1) * rows]
-                keep = (h == p) if mine else (h != p)
-
-                @pl.when(keep)
-                def _():
-                    q_keep[zz, :, lanes] = block
-
-                @pl.when(jnp.logical_not(keep))
-                def _():
-                    q_out[zz, :, lanes] = block.astype(BF16)
-
-            return 0
-
-        lax.fori_loop(0, cols // SIDE, part_of, 0)
-        for zz, mine in zip(places, in_own):
-
-            @pl.when((h != p) if mine else (h == p))
-            def _():
-                q_copy(zz).start()
-
-    def kv_copy(hh, zz):
-        return remote(
-            kv_out.at[hh, zz],
-            kv_in.at[hh, zz],
-            kv_send.at[hh, zz],
-            kv_recv.at[hh, zz],
-            req=pair,
-        )
-
-    def low_copy(zz):
-        return remote(
-            low_out.at[zz], low_in.at[z], low_send.at[zz], low_recv.at[z], req=h * ring + zz
-        )
-
-    def low_arrival(zz):
-        return remote(
-            low_out.at[zz], low_in.at[zz], low_send.at[zz], low_recv.at[zz], req=h * ring + zz
-        )
-
-    near_lane = lax.broadcasted_iota(jnp.int32, (rows, HEAD), 1) < maps
-    prompt_of = lax.broadcasted_iota(jnp.int32, (rows, HEAD), 0) // SLOTS
-    match = jnp.zeros((rows, HEAD), F32)
-    for i in range(prompts):
-        adapter = adapters[t * prompts + i]
-        mine = jnp.where(adapter == r, 1.0, 0.0)
-        theirs = jnp.where(adapter == across, 1.0, 0.0)
-        match = jnp.where(prompt_of == i, jnp.where(near_lane, mine, theirs), match)
-
-    def finish_kv(hh, zz, total):
-        kv_own[hh, zz] = total
-        kv_out[hh, zz] = total.astype(BF16)
-        kv_copy(hh, zz).start()
-
-    def finish_own(zz, self_too=False):
-        a_copy(zz).wait_recv()
-        total = a_own[zz] + a_in[zz].astype(F32)
-        finish_kv(h, zz, total[:, :HEAD])
-        low = jnp.where(match > 0.0, total[:, HEAD:SIDE], 0.0)
-        low = low + pltpu.roll(low, HEAD // 2, 1)
-        packed = jnp.where(near_lane[:part], low[:part], low[part:]).astype(BF16)
-        if self_too:
-            low_in[zz] = packed
-        else:
-            low_out[zz] = packed
-            low_copy(zz).start()
-
-    def finish_cross(zz):
-        b_copy(zz).wait_recv()
-        finish_kv(1 - h, zz, b_own[zz] + b_in[zz].astype(F32))
-
-    def ahead(k):
-        return [(z + ring - k) % ring, (z + k) % ring]
-
-    def arrive_own(k):
-        for way, s in order:
-            arrive(own(k, way), s)
-            src = piece(own(k, way), s)
-            if k < half - 1:
-                hop(own(k + 1, way), s, src, toward[way]).start()
-            elif s == way:
-                hop(own(half), s, src, toward[way]).start()
-            if k == 1:
-                hop(cross(k, way), s, src, across).start()
-
-    def arrive_cross(k):
-        for way, s in order:
-            arrive(cross(k, way), s)
-            src = piece(cross(k, way), s)
-            if k < half - 1:
-                hop(cross(k + 1, way), s, src, toward[way]).start()
-
-    def arrive_both(b):
-        for s in range(2):
-            arrive(b, s)
-
     def make_messages():
         steps = sq.shape[1]
         msg_f32[...] = jnp.zeros(msg_f32.shape, F32)
@@ -372,6 +227,172 @@
                 msg_f32[i, first + SLOTS : first + SLOTS + 1] = new[1:2]
         msg_ref[...] = msg_f32[...].astype(BF16)
 
+    for i in range(prompts):
+        uv_out[i] = uv[adapters[t * prompts + i]]
+    uv_copy = remote(uv_out, uv_in, uv_sems.at[0], uv_sems.at[1], req=pair)
+    uv_copy.start()
+    make_messages()
+
+    map_hop().wait_recv()
+    for o in range(1, tp_count):
+        map_spread((t + o) % tp_count, t).start()
+
+    def q_copy(zz):
+        return remote(q_out.at[zz], q_in.at[zz], q_send.at[zz], q_recv.at[zz], pp=other)
+
+    def a_copy(zz):
+        return remote(a_out.at[zz], a_in.at[zz], a_send.at[zz], a_recv.at[zz], pp=other)
+
+    def b_copy(zz):
+        return remote(b_out.at[zz], b_in.at[zz], b_send.at[zz], b_recv.at[zz], pp=other)
+
+    def late_copy(i, d):
+        return remote(
+            b_out.at[ahead(half - 1)[d]],
+            late_in.at[i, d],
+            late_send.at[i, d],
+            late_recv.at[i, d],
+            req=pair,
+            pp=(p, other)[i],
+        )
+
+    def project(first, places, in_own, late=False):
+        count = len(places) * rows
+        at = pl.ds(first * rows, count)
+        side = SIDE if any(in_own) else HEAD
+        got = lax.dot_general(
+            blocks[at, :],
+            side_w[:side],
+            (((1,), (1,)), ((), ())),
+            preferred_element_type=F32,
+        )
+        for i, (zz, mine) in enumerate(zip(places, in_own)):
+            block = got[i * rows : (i + 1) * rows]
+            if mine:
+                a_own[zz] = block
+                a_out[zz] = block.astype(BF16)
+                a_copy(zz).start()
+            else:
+                b_own[zz] = block[:, :HEAD]
+                b_out[zz] = block[:, :HEAD].astype(BF16)
+                b_copy(zz).start()
+                if late:
+                    late_copy(0, i).start()
+                    late_copy(1, i).start()
+
+        def part_of(n, _):
+            lanes = pl.ds(pl.multiple_of(n * SIDE, SIDE), SIDE)
+            got = jnp.dot(blocks[at, :], weights[:, lanes], preferred_element_type=F32)
+            for i, (zz, mine) in enumerate(zip(places, in_own)):
+                block = got[i * rows : (i + 1) * rows]
+                keep = (h == p) if mine else (h != p)
+
+                @pl.when(keep)
+                def _():
+                    q_keep[zz, :, lanes] = block
+
+                @pl.when(jnp.logical_not(keep))
+                def _():
+                    q_out[zz, :, lanes] = block.astype(BF16)
+
+            return 0
+
+        lax.fori_loop(0, cols // SIDE, part_of, 0)
+        for zz, mine in zip(places, in_own):
+
+            @pl.when((h != p) if mine else (h == p))
+            def _():
+                q_copy(zz).start()
+
+    def kv_copy(hh, zz):
+        return remote(
+            kv_out.at[hh, zz],
+            kv_in.at[hh, zz],
+            kv_send.at[hh, zz],
+            kv_recv.at[hh, zz],
+            req=pair,
+        )
+
+    def low_copy(zz):
+        return remote(
+            low_out.at[zz], low_in.at[z], low_send.at[zz], low_recv.at[z], req=h * ring + zz
+        )
+
+    def low_arrival(zz):
+        return remote(
+            low_out.at[zz], low_in.at[zz], low_send.at[zz], low_recv.at[zz], req=h * ring + zz
+        )
+
+    near_lane = lax.broadcasted_iota(jnp.int32, (rows, HEAD), 1) < maps
+    prompt_of = lax.broadcasted_iota(jnp.int32, (rows, HEAD), 0) // SLOTS
+    match = jnp.zeros((rows, HEAD), F32)
+    for i in range(prompts):
+        adapter = adapters[t * prompts + i]
+        mine = jnp.where(adapter == r, 1.0, 0.0)
+        theirs = jnp.where(adapter == across, 1.0, 0.0)
+        match = jnp.where(prompt_of == i, jnp.where(near_lane, mine, theirs), match)
+
+    def finish_kv(hh, zz, total):
+        kv_own[hh, zz] = total
+        kv_out[hh, zz] = total.astype(BF16)
+        kv_copy(hh, zz).start()
+
+    def finish_own(zz, self_too=False):
+        a_copy(zz).wait_recv()
+        total = a_own[zz] + a_in[zz].astype(F32)
+        finish_kv(h, zz, total[:, :HEAD])
+        low = jnp.where(match > 0.0, total[:, HEAD:SIDE], 0.0)
+        low = low + pltpu.roll(low, HEAD // 2, 1)
+        packed = jnp.where(near_lane[:part], low[:part], low[part:]).astype(BF16)
+        if self_too:
+            low_in[zz] = packed
+        else:
+            low_out[zz] = packed
+            low_copy(zz).start()
+
+    def finish_cross(zz):
+        b_copy(zz).wait_recv()
+        finish_kv(1 - h, zz, b_own[zz] + b_in[zz].astype(F32))
+
+    def ahead(k):
+        return [(z + ring - k) % ring, (z + k) % ring]
+
+    def arrive_own(k):
+        for way, s in order:
+            arrive(own(k, way), s)
+            src = piece(own(k, way), s)
+            if k < half - 1:
+                hop(own(k + 1, way), s, src, toward[way]).start()
+            elif s == way:
+                hop(own(half), s, src, toward[way]).start()
+            if k == 1:
+                hop(cross(k, way), s, src, across).start()
+
+    def arrive_cross(k, which=order):
+        for way, s in which:
+            arrive(cross(k, way), s)
+            src = piece(cross(k, way), s)
+            if k < half - 1:
+                hop(cross(k + 1, way), s, src, toward[way]).start()
+
+    def arrive_both(b):
+        for s in range(2):
+            arrive(b, s)
+
+    def step_copy(i):
+        target = t * per_dev + i
+        return remote(
+            msg_ref.at[i],
+            step_in.at[r % per_dev],
+            step_send.at[i],
+            step_got.at[r % per_dev],
+            req=target,
+            tp=r // per_dev,
+        )
+
+    def step_self(i):
+        return (t * per_dev + i == r) & (r // per_dev == t)
+
     both = [True, True]
     neither = [False, False]
 
@@ -384,43 +405,45 @@
     project(0, [z, z], [True, False])
     if half > 2:
         project(own(1), ahead(1), both)
-    make_messages()
     for k in range(3, half):
         arrive_own(k)
         arrive_cross(k - 2)
-        if k == 3:
-            finish_own(z, True)
-            finish_cross(z)
         project(own(k - 1), ahead(k - 1), both)
-        project(cross(k - 2), ahead(k - 2), neither)
-        for zz in ahead(k - 2):
-            finish_own(zz)
-    for i in range(prompts):
-        uv_out[i] = uv[adapters[t * prompts + i]]
-    uv_copy = remote(uv_out, uv_in, uv_sems.at[0], uv_sems.at[1], req=pair)
-    uv_copy.start()
+        if k < half - 1:
+            project(cross(k - 2), ahead(k - 2), neither)
     for s in range(2):
         arrive(own(half), s)
         hop(cross(half), s, piece(own(half), s), across).start()
+    pl.semaphore_signal(hello, inc=1, device_id=(across, t, p), device_id_type=MESH)
     project(own(half - 1), ahead(half - 1) + [far], [True] * 3)
+    pl.semaphore_wait(hello, 1)
+    for i in range(per_dev):
+
+        @pl.when(step_self(i))
+        def _():
+            step_in[r % per_dev] = msg_ref[i]
+
+        @pl.when(jnp.logical_not(step_self(i)))
+        def _():
+            step_copy(i).start()
+
+    if half > 3:
+        project(cross(half - 3), ahead(half - 3), neither)
+    finish_own(z, True)
+    finish_cross(z)
+    for k in range(1, half - 1):
+        for zz in ahead(k):
+            finish_own(zz)
     if half > 2:
-        arrive_cross(half - 2)
-        for zz in ahead(half - 2):
-            finish_own(zz)
-        for zz in ahead(half - 1) + [far]:
-            finish_own(zz)
+        arrive_cross(half - 2, order[:2])
+    for zz in ahead(half - 1) + [far]:
+        finish_own(zz)
+    if half > 2:
+        arrive_cross(half - 2, order[2:])
         project(cross(half - 2), ahead(half - 2), neither)
-        if half > 3:
-            for zz in ahead(half - 3):
-                finish_cross(zz)
-        else:
-            finish_own(z, True)
-            finish_cross(z)
-    else:
-        finish_own(z, True)
-        finish_cross(z)
-        for zz in ahead(half - 1) + [far]:
-            finish_own(zz)
+    for k in range(1, half - 2):
+        for zz in ahead(k):
+            finish_cross(zz)
     arrive_both(cross(half))
     project(cross(half), [far], [False])
 
@@ -453,30 +476,6 @@
             finish_cross(zz)
     arrive_cross(half - 1)
     project(cross(half - 1), ahead(half - 1), neither, late=True)
-
-    def step_copy(i):
-        target = t * per_dev + i
-        return remote(
-            msg_ref.at[i],
-            step_in.at[r % per_dev],
-            step_send.at[i],
-            step_got.at[r % per_dev],
-            req=target,
-            tp=r // per_dev,
-        )
-
-    def step_self(i):
-        return (t * per_dev + i == r) & (r // per_dev == t)
-
-    for i in range(per_dev):
-
-        @pl.when(step_self(i))
-        def _():
-            step_in[r % per_dev] = msg_ref[i]
-
-        @pl.when(jnp.logical_not(step_self(i)))
-        def _():
-            step_copy(i).start()
 
     finish_cross(far)
     for zz in ahead(half - 1):
@@ -794,6 +793,7 @@
             dma((per_dev,)),
             dma((per_dev, tp_count)),
             dma((req_count,)),
+            pltpu.SemaphoreType.REGULAR,
         ],
         compiler_params=pltpu.CompilerParams(
             collective_id=0, has_side_effects=True, vmem_limit_bytes=56 * 1024 * 1024

time: 69.2 us -> 67.1 us (0.970)
  Pallas kernels: 68.4 us -> 66.3 us
    pallas_call x1, Pallas kernels: 66.7 us -> 64.6 us  [local(): pl.pallas_call(functools.partial(kernel, req_count, tp_count), out_shape=...]
where the time goes in v5:
time: 67.1 us; the launch traced here: 66.9 us
  Pallas kernels  66.3 us (99%)
    pallas_call x1, Pallas kernels, local(): pl.pallas_call(functools.partial(kernel, req_count, tp_count), out_shape=...  64.6 us
    pallas_call x1, Pallas kernels, local(): pl.pallas_call(deliver, out_shape=(jax.ShapeDtypeStruct(prefill.shape, BF...  1.7 us

profile of v5, /device:TPU:1, one launch (start us, length us, event | category | flops | bytes accessed | tf_op | source)
XLA Modules:
  0.0 66.9 jit_solution(4003107518257268597)
XLA Ops:
  0.6 64.6 %shard_map.131 = (bf16[4,64,512]{2,1,0:T(8,128)(2,1)}, bf16[16,16,128]{2,1,0:T(8,128)(2,1)}) custom-call(s32[32]{0:T(128)} %lens.1, s32[32]{0:T(128)} %adapters.1, bf16[32,4096]{1,0:T(8,128)(2,1)} %bitcast.11, bf16[4096,512]{1,0:T(8,128)(2,1)} %wq_hbm.1, bf16[64,4096]{1,0:T(8,128)(2,1)} %bitcast.9, bf16[64,4096]{1,0:T(8,128)(2,1)} %bitcast.10, ...), custom_call_target="tpu_custom_call" | custom-call | flops 3221225472 | bytes 6291456 | tf_op jit(solution)/shard_map/pallas_call | solution.py:729
  65.2 1.7 %shard_map.132 = (bf16[4,64,512]{2,1,0:T(8,128)(2,1)}, bf16[1,4,8192]{2,1,0:T(4,128)(2,1)}) custom-call(bf16[4,64,512]{2,1,0:T(8,128)(2,1)} %get-tuple-element.4.prefill_in, bf16[16,16,128]{2,1,0:T(8,128)(2,1)} %get-tuple-element.5.decoded_in), custom_call_target="tpu_custom_call" | custom-call | tf_op jit(solution)/shard_map/pallas_call | solution.py:820

commit v6 on v5

--- a/solution.py
+++ b/solution.py
@@ -58,6 +58,7 @@
     late_in,
     low_out,
     low_in,
+    far_in,
     rank_all,
     ranks,
     uv_out,
@@ -84,6 +85,8 @@
     late_recv,
     low_send,
     low_recv,
+    far_send,
+    far_recv,
     rank_send,
     rank_recv,
     uv_sems,
@@ -92,6 +95,8 @@
     out_send,
     out_got,
     hello,
+    prefill,
+    prefill_sem,
 ):
     r, t, p = lax.axis_index("req"), lax.axis_index("tp"), lax.axis_index("pp")
     ring = req_count // 2
@@ -256,7 +261,43 @@
             pp=(p, other)[i],
         )
 
-    def project(first, places, in_own, late=False):
+    def low_copy(zz):
+        return remote(
+            low_out.at[zz], low_in.at[z], low_send.at[zz], low_recv.at[z], req=h * ring + zz
+        )
+
+    def low_arrival(zz):
+        return remote(
+            low_out.at[zz], low_in.at[zz], low_send.at[zz], low_recv.at[zz], req=h * ring + zz
+        )
+
+    def far_low(zz, source):
+        return remote(
+            low_out.at[zz],
+            far_in.at[source],
+            far_send.at[zz],
+            far_recv.at[source],
+            req=h * ring + zz,
+            pp=other,
+        )
+
+    near_lane = lax.broadcasted_iota(jnp.int32, (rows, HEAD), 1) < maps
+    prompt_of = lax.broadcasted_iota(jnp.int32, (rows, HEAD), 0) // SLOTS
+    match = jnp.zeros((rows, HEAD), F32)
+    for i in range(prompts):
+        adapter = adapters[t * prompts + i]
+        mine = jnp.where(adapter == r, 1.0, 0.0)
+        theirs = jnp.where(adapter == across, 1.0, 0.0)
+        match = jnp.where(prompt_of == i, jnp.where(near_lane, mine, theirs), match)
+
+    def packed_low(both_maps):
+        low = jnp.where(match > 0.0, both_maps, 0.0)
+        low = low + pltpu.roll(low, HEAD // 2, 1)
+        return jnp.where(near_lane[:part], low[:part], low[part:]).astype(BF16)
+
+    waiting = []
+
+    def project(first, places, in_own, late=False, far_ranks=False):
         count = len(places) * rows
         at = pl.ds(first * rows, count)
         side = SIDE if any(in_own) else HEAD
@@ -271,6 +312,10 @@
             if mine:
                 a_own[zz] = block
                 a_out[zz] = block.astype(BF16)
+                if far_ranks:
+                    low_out[zz] = packed_low(block[:, HEAD:])
+                    low_copy(zz).start()
+                    far_low(zz, z).start()
                 a_copy(zz).start()
             else:
                 b_own[zz] = block[:, :HEAD]
@@ -299,10 +344,14 @@
 
         lax.fori_loop(0, cols // SIDE, part_of, 0)
         for zz, mine in zip(places, in_own):
-
-            @pl.when((h != p) if mine else (h == p))
-            def _():
-                q_copy(zz).start()
+            if False:
+
+                @pl.when((h != p) if mine else (h == p))
+                def _():
+                    q_copy(zz).start()
+
+            else:
+                waiting.append((zz, mine))
 
     def kv_copy(hh, zz):
         return remote(
@@ -313,41 +362,19 @@
             req=pair,
         )
 
-    def low_copy(zz):
-        return remote(
-            low_out.at[zz], low_in.at[z], low_send.at[zz], low_recv.at[z], req=h * ring + zz
-        )
-
-    def low_arrival(zz):
-        return remote(
-            low_out.at[zz], low_in.at[zz], low_send.at[zz], low_recv.at[zz], req=h * ring + zz
-        )
-
-    near_lane = lax.broadcasted_iota(jnp.int32, (rows, HEAD), 1) < maps
-    prompt_of = lax.broadcasted_iota(jnp.int32, (rows, HEAD), 0) // SLOTS
-    match = jnp.zeros((rows, HEAD), F32)
-    for i in range(prompts):
-        adapter = adapters[t * prompts + i]
-        mine = jnp.where(adapter == r, 1.0, 0.0)
-        theirs = jnp.where(adapter == across, 1.0, 0.0)
-        match = jnp.where(prompt_of == i, jnp.where(near_lane, mine, theirs), match)
-
     def finish_kv(hh, zz, total):
         kv_own[hh, zz] = total
         kv_out[hh, zz] = total.astype(BF16)
         kv_copy(hh, zz).start()
 
-    def finish_own(zz, self_too=False):
+    def finish_own(zz, self_too=False, sent=False):
         a_copy(zz).wait_recv()
         total = a_own[zz] + a_in[zz].astype(F32)
         finish_kv(h, zz, total[:, :HEAD])
-        low = jnp.where(match > 0.0, total[:, HEAD:SIDE], 0.0)
-        low = low + pltpu.roll(low, HEAD // 2, 1)
-        packed = jnp.where(near_lane[:part], low[:part], low[part:]).astype(BF16)
         if self_too:
-            low_in[zz] = packed
-        else:
-            low_out[zz] = packed
+            low_in[zz] = packed_low(total[:, HEAD:SIDE])
+        elif not sent:
+            low_out[zz] = packed_low(total[:, HEAD:SIDE])
             low_copy(zz).start()
 
     def finish_cross(zz):
@@ -415,7 +442,7 @@
         arrive(own(half), s)
         hop(cross(half), s, piece(own(half), s), across).start()
     pl.semaphore_signal(hello, inc=1, device_id=(across, t, p), device_id_type=MESH)
-    project(own(half - 1), ahead(half - 1) + [far], [True] * 3)
+    project(own(half - 1), ahead(half - 1) + [far], [True] * 3, far_ranks=True)
     pl.semaphore_wait(hello, 1)
     for i in range(per_dev):
 
@@ -437,45 +464,66 @@
     if half > 2:
         arrive_cross(half - 2, order[:2])
     for zz in ahead(half - 1) + [far]:
-        finish_own(zz)
+        finish_own(zz, sent=True)
     if half > 2:
         arrive_cross(half - 2, order[2:])
         project(cross(half - 2), ahead(half - 2), neither)
+
+    distances = sorted(range(ring), key=lambda o: -min(o, ring - o))
+
+    def others(body):
+        for o in distances:
+            body((1 - h) * ring + (z + o) % ring)
+            if o > 0:
+                body(h * ring + (z + o) % ring)
+
+    def column(body):
+        for o in distances[:-1]:
+            body((z + o) % ring)
+
+    def rank_copy(target, slot):
+        return remote(
+            rank_all.at[slot], rank_all.at[slot], rank_send.at[target], rank_recv.at[slot], req=target
+        )
+
+    column(lambda zz: low_arrival(zz).wait_recv())
+    for zz in ahead(half - 1) + [far]:
+        far_low(zz, zz).wait_recv()
+    low = low_in[0].astype(F32)
+    for zz in range(1, ring):
+        low = low + low_in[zz].astype(F32)
+    for zz in ahead(half - 1) + [far]:
+        low = low + far_in[zz].astype(F32)
+    rank_all[r] = low.astype(BF16)
+    others(lambda target: rank_copy(target, r).start())
+
     for k in range(1, half - 2):
         for zz in ahead(k):
             finish_cross(zz)
     arrive_both(cross(half))
     project(cross(half), [far], [False])
 
-    distances = sorted(range(ring), key=lambda o: -min(o, ring - o))
-
-    def others(body):
-        for o in distances:
-            body((1 - h) * ring + (z + o) % ring)
-            if o > 0:
-                body(h * ring + (z + o) % ring)
-
-    def column(body):
-        for o in distances[:-1]:
-            body((z + o) % ring)
-
-    def rank_copy(target, slot):
-        return remote(
-            rank_all.at[slot], rank_all.at[slot], rank_send.at[target], rank_recv.at[slot], req=target
-        )
-
-    column(lambda zz: low_arrival(zz).wait_recv())
-    low = low_in[0].astype(F32)
-    for zz in range(1, ring):
-        low = low + low_in[zz].astype(F32)
-    rank_all[r] = low.astype(BF16)
-    others(lambda target: rank_copy(target, r).start())
-
     if half > 2:
         for zz in ahead(half - 2):
             finish_cross(zz)
+    def take_pair(hh, zz):
+        kv_copy(hh, zz).wait_recv()
+        kv_oth[hh, zz] = kv_in[hh, zz].astype(F32)
+
+    uv_copy.wait_recv()
+    for o in range(ring):
+        take_pair(h, (z + o) % ring)
+    for o in (0, 1, ring - 1):
+        if o not in (half - 1, half + 1):
+            take_pair(1 - h, (pair + o) % ring)
     arrive_cross(half - 1)
     project(cross(half - 1), ahead(half - 1), neither, late=True)
+    for zz, mine in waiting:
+
+        @pl.when((h != p) if mine else (h == p))
+        def _():
+            q_copy(zz).start()
+
 
     finish_cross(far)
     for zz in ahead(half - 1):
@@ -484,24 +532,11 @@
     for i in range(2):
         for d in range(2):
             late_copy(i, d).wait_recv()
-    uv_copy.wait_recv()
-    for hh in range(2):
-        for zz in range(ring):
-            there = [(hh == 1 - h) & (zz == late_zz) for late_zz in pair_late]
-
-            @pl.when(jnp.logical_not(there[0] | there[1]))
-            def _():
-                kv_copy(hh, zz).wait_recv()
-                kv_oth[hh, zz] = kv_in[hh, zz].astype(F32)
-
     for d in range(2):
         kv_oth[1 - h, pair_late[d]] = late_in[0, d].astype(F32) + late_in[1, d].astype(F32)
-
-    others(lambda source: rank_copy(source, source).wait_recv())
-    for source in range(req_count):
-        packed = rank_all[source].astype(F32)
-        ranks[source, :part] = packed
-        ranks[source, part:] = pltpu.roll(packed, HEAD // 2, 1)
+    for o in range(2, ring - 1):
+        if o not in (half - 1, half + 1):
+            take_pair(1 - h, (pair + o) % ring)
 
     even = r % 2 == 0
     slots = req_count * SLOTS
@@ -509,22 +544,27 @@
     low_lane = lax.broadcasted_iota(jnp.int32, (slots, HEAD), 1) < HEAD // 2
     scale = HEAD ** (-0.5)
 
-    def assemble(n):
+    def halves(n):
         at = pl.ds(pl.multiple_of(n * SLOTS, SLOTS), SLOTS)
         mine = kv_own[:, :, at, :].reshape(slots, HEAD)
         theirs = kv_oth[:, :, at, :].reshape(slots, HEAD)
-        first = jnp.where(even, mine, theirs)
-        second = jnp.where(even, theirs, mine)
-        k = jnp.where(low_lane, first, pltpu.roll(second, HEAD // 2, 1)).astype(BF16)
+        return jnp.where(even, mine, theirs), jnp.where(even, theirs, mine)
+
+    def keys_of(n):
+        first, second = halves(n)
+        return jnp.where(low_lane, first, pltpu.roll(second, HEAD // 2, 1)).astype(BF16)
+
+    def values_of(n):
+        first, second = halves(n)
         v = jnp.where(low_lane, pltpu.roll(first, HEAD // 2, 1), second)
         uv_mine, uv_theirs = uv_out[n], uv_in[n]
         up_v = jnp.concatenate(
             [jnp.where(even, uv_mine, uv_theirs), jnp.where(even, uv_theirs, uv_mine)], axis=1
         )
+        at = pl.ds(pl.multiple_of(n * SLOTS, SLOTS), SLOTS)
         rank_rows = ranks[:, at, :].reshape(slots, HEAD).astype(BF16)
         v = v + jnp.dot(rank_rows[:, rank:maps], up_v, preferred_element_type=F32)
-        k_full[n] = k
-        v_full[n] = v.astype(BF16)
+        return v.astype(BF16)
 
     steps = step_out.shape[1] // heads
     qrows = heads * steps
@@ -566,10 +606,12 @@
         def _():
             step_arrival(j).wait_recv()
 
+    weighed = []
+    for j in range(per_dev):
         n = 2 * j + p
-        assemble(n)
         length = lens[t * prompts + n]
-        k, v = k_full[n], v_full[n]
+        k = keys_of(n)
+        k_full[n] = k
         got = step_in[j]
         qs = got[:qrows]
         tail = got[qrows:].astype(F32)
@@ -588,15 +630,30 @@
         )
         e_old, e_new = jnp.exp(s_old - top), jnp.exp(s_new - top)
         total = jnp.sum(e_old, axis=1, keepdims=True) + jnp.sum(e_new, axis=1, keepdims=True)
-        mixed = jnp.zeros((qrows, HEAD), F32)
-        for e, values in ((e_old, v), (e_new, new_v)):
+
+        def weigh(e, values):
             coarse = e.astype(BF16)
             fine = (e - coarse.astype(F32)).astype(BF16)
-            mixed = mixed + jnp.dot(coarse, values, preferred_element_type=F32)
-            mixed = mixed + jnp.dot(fine, values, preferred_element_type=F32)
-        step_out[j] = (mixed / total).astype(BF16)
-        for o in sorted(range(tp_count), key=lambda o: -min(o, tp_count - o)):
-            target = (t + o) % tp_count
+            return jnp.dot(coarse, values, preferred_element_type=F32) + jnp.dot(
+                fine, values, preferred_element_type=F32
+            )
+
+        weighed.append((weigh, e_old, weigh(e_new, new_v), 1.0 / total))
+
+    others(lambda source: rank_copy(source, source).wait_recv())
+    for source in range(req_count):
+        packed = rank_all[source].astype(F32)
+        ranks[source, :part] = packed
+        ranks[source, part:] = pltpu.roll(packed, HEAD // 2, 1)
+    for j in range(per_dev):
+        n = 2 * j + p
+        v = values_of(n)
+        v_full[n] = v
+        weigh, e_old, new_part, inverse = weighed[j]
+        step_out[j] = ((weigh(e_old, v) + new_part) * inverse).astype(BF16)
+    for o in sorted(range(tp_count), key=lambda o: -min(o, tp_count - o)):
+        target = (t + o) % tp_count
+        for j in range(per_dev):
             if o == 0:
 
                 @pl.when(t * per_dev + j == r)
@@ -610,7 +667,9 @@
                 out_copy(j, target).start()
 
     for j in range(per_dev):
-        assemble(2 * j + 1 - p)
+        n = 2 * j + 1 - p
+        k_full[n] = keys_of(n)
+        v_full[n] = values_of(n)
     for zz in range(ring):
         q_copy(zz).wait_recv()
     base_q = (q_keep[...] + q_in[...].astype(F32)).reshape(ring, prompts, SLOTS, cols)
@@ -618,6 +677,9 @@
     row_pos = lax.broadcasted_iota(jnp.int32, (heads * share, slots), 0) % share + p * share
     col_pos = lax.broadcasted_iota(jnp.int32, (heads * share, slots), 1)
     out_pos = lax.broadcasted_iota(jnp.int32, (heads * share, HEAD), 0) % share + p * share
+    def prefill_copy(i):
+        return pltpu.make_async_copy(prefill.at[i], prefill_ref.at[i], prefill_sem.at[i])
+
     for i in range(prompts):
         length = lens[t * prompts + i]
         adapter = adapters[t * prompts + i]
@@ -635,7 +697,8 @@
         o = jnp.dot(w, v, preferred_element_type=F32)
         o = jnp.where(out_pos < length, o, 0.0).astype(BF16)
         for g in range(heads):
-            prefill_ref[i, :, g * HEAD : (g + 1) * HEAD] = o[g * share : (g + 1) * share]
+            prefill[i, :, g * HEAD : (g + 1) * HEAD] = o[g * share : (g + 1) * share]
+        prefill_copy(i).start()
 
     for b in range(1, 2 * ring):
         for s in range(2):
@@ -658,6 +721,8 @@
         for d in range(2):
             late_copy(i, d).wait_send()
     column(lambda zz: low_copy(zz).wait_send())
+    for zz in ahead(half - 1) + [far]:
+        far_low(zz, z).wait_send()
     others(lambda target: rank_copy(target, r).wait_send())
     uv_copy.wait_send()
     for i in range(per_dev):
@@ -682,6 +747,8 @@
 
     lax.fori_loop(0, req_count, got_out, 0)
     decoded_ref[...] = step_recv[...]
+    for i in range(prompts):
+        prefill_copy(i).wait()
 
 
 def deliver(prefill_in, decoded_in, prefill_ref, decoded_ref):
@@ -733,7 +800,7 @@
             jax.ShapeDtypeStruct((req_count, heads * steps, HEAD), BF16),
         ),
         in_specs=[smem, smem] + [hbm] * 10,
-        out_specs=(vmem, vmem),
+        out_specs=(hbm, vmem),
         scratch_shapes=[
             pltpu.VMEM((per_dev, heads * steps + 2 * SLOTS, HEAD), BF16),
             pltpu.VMEM((per_dev, heads * steps + 2 * SLOTS, HEAD), F32),
@@ -758,6 +825,7 @@
             pltpu.VMEM((2, ring, rows, HEAD), BF16),
             pltpu.VMEM((2, ring, rows, HEAD), BF16),
             pltpu.VMEM((2, 2, rows, HEAD), BF16),
+            pltpu.VMEM((ring, rows // 2, HEAD), BF16),
             pltpu.VMEM((ring, rows // 2, HEAD), BF16),
             pltpu.VMEM((ring, rows // 2, HEAD), BF16),
             pltpu.VMEM((req_count, rows // 2, HEAD), BF16),
@@ -786,6 +854,8 @@
             dma((2, 2)),
             dma((ring,)),
             dma((ring,)),
+            dma((ring,)),
+            dma((ring,)),
             dma((req_count,)),
             dma((req_count,)),
             dma((2,)),
@@ -794,6 +864,8 @@
             dma((per_dev, tp_count)),
             dma((req_count,)),
             pltpu.SemaphoreType.REGULAR,
+            pltpu.VMEM((prompts, total_slots // 2, cols), BF16),
+            dma((prompts,)),
         ],
         compiler_params=pltpu.CompilerParams(
             collective_id=0, has_side_effects=True, vmem_limit_bytes=56 * 1024 * 1024

time: 67.1 us -> 66.4 us (0.990)
  Pallas kernels: 66.3 us -> 65.6 us
    pallas_call x1, Pallas kernels: 64.6 us -> 63.9 us  [local(): pl.pallas_call(functools.partial(kernel, req_count, tp_count), out_shape=...]
where the time goes in v6:
time: 66.4 us; the launch traced here: 66.2 us
  Pallas kernels  65.6 us (99%)
    pallas_call x1, Pallas kernels, local(): pl.pallas_call(functools.partial(kernel, req_count, tp_count), out_shape=...  63.9 us
    pallas_call x1, Pallas kernels, local(): pl.pallas_call(deliver, out_shape=(jax.ShapeDtypeStruct(prefill.shape, BF...  1.7 us

profile of v6, /device:TPU:1, one launch (start us, length us, event | category | flops | bytes accessed | tf_op | source)
XLA Modules:
  0.0 66.2 jit_solution(4841833855081905492)
XLA Ops:
  0.6 63.9 %shard_map.131 = (bf16[4,64,512]{2,1,0:T(8,128)(2,1)}, bf16[16,16,128]{2,1,0:T(8,128)(2,1)}) custom-call(s32[32]{0:T(128)} %lens.1, s32[32]{0:T(128)} %adapters.1, bf16[32,4096]{1,0:T(8,128)(2,1)} %bitcast.11, bf16[4096,512]{1,0:T(8,128)(2,1)} %wq_hbm.1, bf16[64,4096]{1,0:T(8,128)(2,1)} %bitcast.9, bf16[64,4096]{1,0:T(8,128)(2,1)} %bitcast.10, ...), custom_call_target="tpu_custom_call" | custom-call | flops 3221225472 | bytes 6291456 | tf_op jit(solution)/shard_map/pallas_call | solution.py:796
  64.5 1.7 %shard_map.132 = (bf16[4,64,512]{2,1,0:T(8,128)(2,1)}, bf16[1,4,8192]{2,1,0:T(4,128)(2,1)}) custom-call(bf16[4,64,512]{2,1,0:T(8,128)(2,1)} %get-tuple-element.4.prefill_in, bf16[16,16,128]{2,1,0:T(8,128)(2,1)} %get-tuple-element.5.decoded_in), custom_call_target="tpu_custom_call" | custom-call | tf_op jit(solution)/shard_map/pallas_call | solution.py:892

commit v7 on v6

--- a/solution.py
+++ b/solution.py
@@ -467,7 +467,6 @@
         finish_own(zz, sent=True)
     if half > 2:
         arrive_cross(half - 2, order[2:])
-        project(cross(half - 2), ahead(half - 2), neither)
 
     distances = sorted(range(ring), key=lambda o: -min(o, ring - o))
 
@@ -496,6 +495,9 @@
         low = low + far_in[zz].astype(F32)
     rank_all[r] = low.astype(BF16)
     others(lambda target: rank_copy(target, r).start())
+
+    if half > 2:
+        project(cross(half - 2), ahead(half - 2), neither)
 
     for k in range(1, half - 2):
         for zz in ahead(k):

time: 66.4 us -> 66.4 us (level)
  no operation moved by 1% of the time
where the time goes in v7:
time: 66.4 us; the launch traced here: 66.2 us
  Pallas kernels  65.6 us (99%)
    pallas_call x1, Pallas kernels, local(): pl.pallas_call(functools.partial(kernel, req_count, tp_count), out_shape=...  63.9 us
    pallas_call x1, Pallas kernels, local(): pl.pallas_call(deliver, out_shape=(jax.ShapeDtypeStruct(prefill.shape, BF...  1.7 us

profile of v7, /device:TPU:1, one launch (start us, length us, event | category | flops | bytes accessed | tf_op | source)
XLA Modules:
  0.0 66.2 jit_solution(5580032664939698810)
XLA Ops:
  0.6 63.9 %shard_map.131 = (bf16[4,64,512]{2,1,0:T(8,128)(2,1)}, bf16[16,16,128]{2,1,0:T(8,128)(2,1)}) custom-call(s32[32]{0:T(128)} %lens.1, s32[32]{0:T(128)} %adapters.1, bf16[32,4096]{1,0:T(8,128)(2,1)} %bitcast.11, bf16[4096,512]{1,0:T(8,128)(2,1)} %wq_hbm.1, bf16[64,4096]{1,0:T(8,128)(2,1)} %bitcast.9, bf16[64,4096]{1,0:T(8,128)(2,1)} %bitcast.10, ...), custom_call_target="tpu_custom_call" | custom-call | flops 3221225472 | bytes 6291456 | tf_op jit(solution)/shard_map/pallas_call | solution.py:798
  64.5 1.7 %shard_map.132 = (bf16[4,64,512]{2,1,0:T(8,128)(2,1)}, bf16[1,4,8192]{2,1,0:T(4,128)(2,1)}) custom-call(bf16[4,64,512]{2,1,0:T(8,128)(2,1)} %get-tuple-element.4.prefill_in, bf16[16,16,128]{2,1,0:T(8,128)(2,1)} %get-tuple-element.5.decoded_in), custom_call_target="tpu_custom_call" | custom-call | tf_op jit(solution)/shard_map/pallas_call | solution.py:894
